TPU v7x, 128 devices: a whole 4x4x4 slice. The times are simulated.
128 devices in a mesh: replica: 4 (over y_lo, core), fsdp: 32 (over y_hi, x, z).
Axes of the slice: x: 4, y: 4 (y_hi: 2, y_lo: 2; y = y_hi * 2 + y_lo), z: 4, core: 2. Of those that a mesh axis runs over, the one named last changes fastest.
Arguments:
- activations: bfloat16 [4, 16384, 4096], P('replica', 'fsdp'), may hold values from -6 to 6
- kv_cotangent: bfloat16 [4, 16384, 1024], P('replica', 'fsdp'), may hold values from -6 to 6
- kv_master: float32 [4, 4096, 1024], P('replica', 'fsdp'), may hold values from -0.09375 to 0.09375
- kv_first: float32 [4, 4096, 1024], P('replica', 'fsdp'), may hold values from -6 to 6
- kv_second: float32 [4, 4096, 1024], P('replica', 'fsdp'), may hold values from 0.25 to 4
- outer_params: float32 [2, 1024, 4096], P(None, 'fsdp'), may hold values from -6 to 6
- local_params: float32 [4, 2, 1024, 4096], P('replica', None, 'fsdp'), may hold values from -6 to 6
- outer_momentum: float32 [2, 1024, 4096], P(None, 'fsdp'), may hold values from -6 to 6
Outputs:
- kv_output: bfloat16 [4, 16384, 1024], P('replica', 'fsdp')
- input_grad: bfloat16 [4, 16384, 4096], P('replica', 'fsdp')
- new_master: float32 [4, 4096, 1024], P('replica', 'fsdp')
- new_first: float32 [4, 4096, 1024], P('replica', 'fsdp')
- new_second: float32 [4, 4096, 1024], P('replica', 'fsdp')
- new_outer: float32 [2, 1024, 4096], P(None, 'fsdp')
- new_momentum: float32 [2, 1024, 4096], P(None, 'fsdp')
All inputs are finite; a program needn't handle non-finite values.
Results may differ from a plain program's by a relative error of at most 0.019.
Values may be sent and summed in bfloat16 or wider, within the bound.
A program may use at most 128 MiB of HBM per device.

v0:
```python
import math

import jax
import jax.numpy as jnp
from jax import lax
from jax.sharding import PartitionSpec as P

FIRST_DECAY = 0.9
SECOND_DECAY = 0.95
ADAM_STEPS = 20.0
ADAM_EPSILON = 1e-08
INNER_RATE = 0.01
WEIGHT_DECAY = 0.1
NESTEROV = 0.9
OUTER_RATE = 0.7


def adam_update(master, first, second, grad):
    first = FIRST_DECAY * first + (1.0 - FIRST_DECAY) * grad
    second = SECOND_DECAY * second + (1.0 - SECOND_DECAY) * grad * grad
    first_fix = 1.0 - FIRST_DECAY**ADAM_STEPS
    second_fix = 1.0 - SECOND_DECAY**ADAM_STEPS
    update = first / first_fix / (jnp.sqrt(second / second_fix) + ADAM_EPSILON)
    master = master - INNER_RATE * (update + WEIGHT_DECAY * master)
    return (master, first, second)


def shards(
    activations,
    kv_cotangent,
    kv_master,
    kv_first,
    kv_second,
    outer_params,
    local_params,
    outer_momentum,
):
    tok_rows = activations[0]
    cotangent = kv_cotangent[0]
    master = kv_master[0]
    weights = master.astype(jnp.bfloat16)
    columns = tok_rows
    projected = jnp.dot(
        columns,
        lax.all_gather(weights, "fsdp", axis=0, tiled=True),
        preferred_element_type=jnp.float32,
    )
    input_grad = jnp.einsum(
        "tk,dk->td",
        cotangent,
        lax.all_gather(weights, "fsdp", axis=0, tiled=True),
        preferred_element_type=jnp.float32,
    )
    columns = tok_rows
    summed = lax.psum_scatter(
        jnp.einsum("td,tk->dk", columns, cotangent, preferred_element_type=jnp.float32).astype(
            jnp.bfloat16
        ),
        "fsdp",
        scatter_dimension=0,
        tiled=True,
    ).astype(jnp.float32)
    all_tokens = tok_rows.shape[0] * lax.axis_size("fsdp")
    grad = summed * (1.0 / math.sqrt(all_tokens))
    new_master, new_first, new_second = adam_update(master, kv_first[0], kv_second[0], grad)
    pseudo = outer_params - local_params[0]
    replicas = lax.axis_size("replica")
    summed_pseudo = lax.psum(pseudo.astype(jnp.bfloat16), "replica").astype(jnp.float32)
    mean = summed_pseudo / replicas
    new_momentum = NESTEROV * outer_momentum + mean
    new_outer = outer_params - OUTER_RATE * (mean + NESTEROV * new_momentum)
    return (
        projected.astype(jnp.bfloat16)[None],
        input_grad.astype(jnp.bfloat16)[None],
        new_master[None],
        new_first[None],
        new_second[None],
        new_outer,
        new_momentum,
    )


def solution(mesh):
    placed = (
        P("replica", "fsdp", None),
        P("replica", "fsdp", None),
        P("replica", "fsdp", None),
        P("replica", "fsdp", None),
        P("replica", "fsdp", None),
        P(None, "fsdp", None),
        P("replica", None, "fsdp", None),
        P(None, "fsdp", None),
    )
    return jax.shard_map(
        shards,
        mesh=mesh,
        in_specs=placed,
        out_specs=(
            P("replica", "fsdp", None),
            P("replica", "fsdp", None),
            P("replica", "fsdp", None),
            P("replica", "fsdp", None),
            P("replica", "fsdp", None),
            P(None, "fsdp", None),
            P(None, "fsdp", None),
        ),
        check_vma=False,
    )
```

profile of v0, /device:TPU:0, one launch (start us, length us, event | category | flops | bytes accessed | tf_op | source)
XLA Modules:
  0.0 335.5 jit_solution(5951607894304049223)
XLA Ops:
  8.0 0.0 copy-start
  8.0 0.0 all-reduce.2.cloned.1.call-start
  8.1 2.5 fusion.10
  10.6 0.0 all-reduce.2.cloned.1.call-update
  10.6 0.0 all-gather.2.cloned.1.call-start
  10.6 1.8 bitcast_convert_fusion
  12.4 0.0 all-gather.2.cloned.1.call-update
  12.5 0.0 reduce-scatter.2.cloned.1.call-start
  12.5 0.0 copy-done
  12.5 9.0 %convolution_convert_fusion = bf16[4096,1024]{1,0:T(8,128)(2,1)} fusion(bf16[1,512,4096]{2,1,0:T(8,128)(2,1)} %param.8, bf16[1,512,1024]{2,1,0:T(8,128)(2,1)S(1)} %copy-done), kind=kOutput, calls=%fused_computation | convolution fusion | flops 4299161600 | bytes 13631488 | tf_op jit(solution)/shard_map/td,tk->dk/dot_general | solution.py:56
  21.5 0.0 reduce-scatter.2.cloned.1.call-update
  21.6 38.9 %all-reduce.2.cloned.1.call-done = bf16[2,32,4096]{2,1,0:T(8,128)(2,1)} async-done(((bf16[2,32,4096]{2,1,0:T(8,128)(2,1)}), bf16[2,32,4096]{2,1,0:T(8,128)(2,1)}) %all-reduce.2.cloned.1.call-update) | async-done | bytes 524304 | tf_op jit(solution)/shard_map/psum | solution.py:68
  60.5 0.0 copy-done.1
  60.5 0.0 copy-done.3
  60.5 2.6 multiply_subtract_fusion
  63.1 59.5 %all-gather.2.cloned.1.call-done = bf16[4096,1024]{1,0:T(8,128)(2,1)} async-done(((bf16[128,1024]{1,0:T(8,128)(2,1)}), bf16[4096,1024]{1,0:T(8,128)(2,1)}) %all-gather.2.cloned.1.call-update) | async-done | bytes 8388624 | tf_op jit(solution)/shard_map/all_gather | solution.py:45
  122.6 9.6 %fusion = bf16[1,512,4096]{2,1,0:T(8,128)(2,1)} fusion(bf16[4096,1024]{1,0:T(8,128)(2,1)} %all-gather.2.cloned.1.call-done, bf16[1,512,1024]{2,1,0:T(8,128)(2,1)S(1)} %copy-done), kind=kOutput, calls=%fused_computation.2 | convolution fusion | flops 4297064448 | bytes 13631488 | tf_op jit(solution)/shard_map/tk,dk->td/dot_general | solution.py:48
  132.2 0.0 copy-done.6
  132.2 0.0 copy-done.7
  132.2 0.0 copy-start.4
  132.3 0.0 copy-start.5
  132.3 5.5 %fusion.7 = bf16[1,512,1024]{2,1,0:T(8,128)(2,1)} fusion(bf16[4096,1024]{1,0:T(8,128)(2,1)S(1)} %copy-done.6, bf16[1,512,4096]{2,1,0:T(8,128)(2,1)S(1)} %copy-done.7), kind=kOutput, calls=%fused_computation.7 | convolution fusion | flops 4295491584 | bytes 13631488 | tf_op jit(solution)/shard_map/dot_general | solution.py:43
  137.8 187.7 %reduce-scatter.2.cloned.1.call-done = bf16[128,1024]{1,0:T(8,128)(2,1)} async-done(((bf16[4096,1024]{1,0:T(8,128)(2,1)}), bf16[128,1024]{1,0:T(8,128)(2,1)}) %reduce-scatter.2.cloned.1.call-update) | async-done | bytes 262160 | tf_op jit(solution)/shard_map/reduce_scatter | solution.py:55
  325.5 2.5 fusion.20
  (8 shorter events, 0.0 us)
Async XLA Ops:
  8.0 4.5 %copy-start = (bf16[1,512,1024]{2,1,0:T(8,128)(2,1)S(1)}, bf16[1,512,1024]{2,1,0:T(8,128)(2,1)}, u32[]{:S(2)}) copy-start(bf16[1,512,1024]{2,1,0:T(8,128)(2,1)} %param.9) | copy-start | bytes 3145732
  8.0 52.4 %all-reduce.2.cloned.1.call-start = ((), (), s32[]{:S(2)}) async-start(), calls=%async_computation.3 | async-start | bytes 1048576 | tf_op jit(solution)/shard_map/psum | solution.py:68
  10.6 112.0 %all-gather.2.cloned.1.call-start = ((), (), s32[]{:S(2)}) async-start(), calls=%async_computation.1 | async-start | bytes 8650752 | tf_op jit(solution)/shard_map/all_gather | solution.py:45
  12.5 313.1 %reduce-scatter.2.cloned.1.call-start = ((), (), s32[]{:S(2)}) async-start(), calls=%async_computation.2 | async-start | bytes 8650752 | tf_op jit(solution)/shard_map/reduce_scatter | solution.py:55
  21.5 38.9 %copy-start.1 = (f32[2,32,4096]{2,1,0:T(8,128)S(1)}, f32[2,32,4096]{2,1,0:T(8,128)}, u32[]{:S(2)}) copy-start(f32[2,32,4096]{2,1,0:T(8,128)} %param.13) | copy-start | bytes 3145732
  21.5 38.9 %copy-start.3 = (f32[2,32,4096]{2,1,0:T(8,128)S(1)}, f32[2,32,4096]{2,1,0:T(8,128)}, u32[]{:S(2)}) copy-start(f32[2,32,4096]{2,1,0:T(8,128)} %param.15) | copy-start | bytes 3145732
  122.6 9.6 %copy-start.6 = (bf16[4096,1024]{1,0:T(8,128)(2,1)S(1)}, bf16[4096,1024]{1,0:T(8,128)(2,1)}, u32[]{:S(2)}) copy-start(bf16[4096,1024]{1,0:T(8,128)(2,1)} %all-gather.2.cloned.1.call-done) | copy-start | bytes 25165828
  122.6 9.6 %copy-start.7 = (bf16[1,512,4096]{2,1,0:T(8,128)(2,1)S(1)}, bf16[1,512,4096]{2,1,0:T(8,128)(2,1)}, u32[]{:S(2)}) copy-start(bf16[1,512,4096]{2,1,0:T(8,128)(2,1)} %param.8) | copy-start | bytes 12582916
  132.2 193.3 %copy-start.2 = (f32[1,128,1024]{2,1,0:T(8,128)S(1)}, f32[1,128,1024]{2,1,0:T(8,128)}, u32[]{:S(2)}) copy-start(f32[1,128,1024]{2,1,0:T(8,128)} %param.10) | copy-start | bytes 1572868
  132.2 193.3 %copy-start.4 = (f32[1,128,1024]{2,1,0:T(8,128)S(1)}, f32[1,128,1024]{2,1,0:T(8,128)}, u32[]{:S(2)}) copy-start(f32[1,128,1024]{2,1,0:T(8,128)} %param.12) | copy-start | bytes 1572868
  132.3 193.3 %copy-start.5 = (f32[1,128,1024]{2,1,0:T(8,128)S(1)}, f32[1,128,1024]{2,1,0:T(8,128)}, u32[]{:S(2)}) copy-start(f32[1,128,1024]{2,1,0:T(8,128)} %param.11) | copy-start | bytes 1572868
Sparse Core Ops, SparseCore 0:
  11.9 48.4 all-reduce.1
Sparse Core Ops, SparseCore 1:
  14.8 107.8 all-gather.1
  124.9 200.6 reduce-scatter.1
where the time goes:
time: 336 us; the launch traced here: 335 us
  waiting for transfers between devices  286 us (85%)
  matrix products  24.1 us (7%)
  between operations  15.5 us (5%)
  other arithmetic  9.43 us (3%)
    reduce_scatter x1, waiting for transfers between devices, shards(): lax.psum_scatter(jnp.einsum('td,tk->dk', columns, cotangent, preferred_el...  188 us
    all_gather x1, waiting for transfers between devices, shards(): lax.all_gather(weights, 'fsdp', axis=0, tiled=True)  59.5 us
    psum x1, waiting for transfers between devices, shards(): lax.psum(pseudo.astype(jnp.bfloat16), 'replica').astype(jnp.float32)  38.9 us
    dot_general x1, matrix products, shards(): jnp.einsum('tk,dk->td', cotangent, lax.all_gather(weights, 'fsdp', axis=0...  9.6 us
    dot_general x1, matrix products, shards(): jnp.einsum('td,tk->dk', columns, cotangent, preferred_element_type=jnp.fl...  9.01 us
  transfers between devices with their start and end apart: 3, of which 3 were waited for; matrix products, arithmetic and copies ran while one was open for 9% of the time, Pallas kernels for 0%

commit v1 on v0

v1 whole, which is shorter than its diff:
```python
import math

import jax
import jax.numpy as jnp
from jax import lax
from jax.experimental import pallas as pl
from jax.experimental.pallas import tpu as pltpu
from jax.sharding import PartitionSpec as P

FIRST_DECAY = 0.9
SECOND_DECAY = 0.95
ADAM_STEPS = 20.0
ADAM_EPSILON = 1e-08
INNER_RATE = 0.01
WEIGHT_DECAY = 0.1
NESTEROV = 0.9
OUTER_RATE = 0.7

BF16 = jnp.bfloat16
F32 = jnp.float32
N = 4
ITEMS = 2 * N
LAG_RQ2 = 1
LAG_RS = 2
LAG_GQ2 = 1
LAG_G = 2
ROUNDS = ITEMS + 2


def adam_update(master, first, second, grad):
    first = FIRST_DECAY * first + (1.0 - FIRST_DECAY) * grad
    second = SECOND_DECAY * second + (1.0 - SECOND_DECAY) * grad * grad
    first_fix = 1.0 - FIRST_DECAY**ADAM_STEPS
    second_fix = 1.0 - SECOND_DECAY**ADAM_STEPS
    update = first / first_fix / (jnp.sqrt(second / second_fix) + ADAM_EPSILON)
    master = master - INNER_RATE * (update + WEIGHT_DECAY * master)
    return (master, first, second)


def train_kernel(
    act_hbm,
    cot_hbm,
    master_hbm,
    out_hbm,
    igrad_hbm,
    grad_ref,
    act,
    cot,
    cot_t,
    master,
    w,
    part,
    got_a,
    got_b,
    got_y,
    got_pa,
    got_pb,
    mine,
    acc,
    out,
    igrad,
    load_sem,
    store_sem,
    gp1_s, gp1_r, gp2_s, gp2_r, gy_s, gy_r, gq1_s, gq1_r, gq2_s, gq2_r,
    rq1_s, rq1_r, rq2_s, rq2_r, ry_s, ry_r, rp1_s, rp1_r, rp2_s, rp2_r,
):
    f = lax.axis_index("fsdp")
    y, x, z = f // 16, (f // 4) % 4, f % 4
    first_of = (x, z)
    last_of = (z, x)
    rows = w.shape[1] // 32
    half = rows // 2
    kv = w.shape[2]
    kh = kv // 2
    cols = N * rows

    def device(yy, xx, zz):
        return (yy * 4 + xx) * 4 + zz

    def block(t, yy, p, q):
        return device(yy, p, q) if t == 0 else device(yy, q, p)

    def along_first(t, step):
        return block(t, y, (first_of[t] + step) % 4, last_of[t])

    def along_last(t, step):
        return block(t, y, first_of[t], (last_of[t] + step) % 4)

    partner = device(1 - y, x, z)

    def send_to(src, dst, ss, rs, target):
        return pltpu.make_async_remote_copy(
            src_ref=src, dst_ref=dst, send_sem=ss, recv_sem=rs,
            device_id={"fsdp": target}, device_id_type=pl.DeviceIdType.MESH,
        )

    def w_at(t, b, part_of=None):
        if part_of is None:
            return w.at[t, pl.ds(pl.multiple_of(b * rows, rows), rows)]
        return w.at[t, pl.ds(pl.multiple_of(b * rows + part_of * half, half), half)]

    def sign(d):
        return 1 if d == 0 else 3

    def gp1(t, d):
        own = w_at(t, f)
        return send_to(own, own, gp1_s.at[t, d], gp1_r.at[t, d], along_first(t, sign(d)))

    def gp2(t, d):
        ref = w_at(t, along_first(t, 4 - sign(d)), d)
        return send_to(ref, ref, gp2_s.at[t, d], gp2_r.at[t, d], along_first(t, sign(d)))

    def gy(t, k):
        ref = w_at(t, along_first(t, k))
        return send_to(ref, ref, gy_s.at[t, k], gy_r.at[t, k], partner)

    def gather_item(t, i):
        plane = (y + i // 4) % 2
        return plane, (first_of[t] + i) % 4

    def gq1(t, i, d):
        plane, p = gather_item(t, i)
        ref = w_at(t, block(t, plane, p, last_of[t]))
        return send_to(ref, ref, gq1_s.at[t, i, d], gq1_r.at[t, i, d], along_last(t, sign(d)))

    def gq2(t, i, d):
        plane, p = gather_item(t, i)
        ref = w_at(t, block(t, plane, p, (last_of[t] + 4 - sign(d)) % 4), d)
        return send_to(ref, ref, gq2_s.at[t, i, d], gq2_r.at[t, i, d], along_last(t, sign(d)))

    def reduce_item(t, i):
        plane = (y + 1 + i // 4) % 2
        return plane, (first_of[t] + i + 1) % 4

    def part_at(t, i, q, part_of=None):
        ref = part.at[t, i, q]
        return ref if part_of is None else ref.at[pl.ds(part_of * kh, kh)]

    def rq1(t, i, d):
        return send_to(
            part_at(t, i, (last_of[t] + 2) % 4, d), got_a.at[t, i, d],
            rq1_s.at[t, i, d], rq1_r.at[t, i, d], along_last(t, sign(d)),
        )

    def rq2(t, i, d):
        return send_to(
            part_at(t, i, (last_of[t] + sign(d)) % 4), got_b.at[t, i, d],
            rq2_s.at[t, i, d], rq2_r.at[t, i, d], along_last(t, sign(d)),
        )

    def ry(t, k):
        return send_to(
            part_at(t, k, last_of[t]), got_y.at[t, k], ry_s.at[t, k], ry_r.at[t, k], partner
        )

    def rp1(t, d):
        return send_to(
            part_at(t, 5, last_of[t], d), got_pa.at[t, d],
            rp1_s.at[t, d], rp1_r.at[t, d], along_first(t, sign(d)),
        )

    def rp2(t, d):
        return send_to(
            part_at(t, 4 if d == 0 else 6, last_of[t]), got_pb.at[t, d],
            rp2_s.at[t, d], rp2_r.at[t, d], along_first(t, sign(d)),
        )

    types = (0, 1)
    ways = (0, 1)

    load_master = pltpu.make_async_copy(master_hbm.at[0], master, load_sem.at[0])
    load_cot = pltpu.make_async_copy(cot_hbm.at[0], cot, load_sem.at[1])
    plane_cols = act.shape[1] // 2

    def load_act(plane, slot):
        at = pl.ds(pl.multiple_of(plane * plane_cols, plane_cols), plane_cols)
        return pltpu.make_async_copy(act_hbm.at[0, :, at], act.at[:, at], load_sem.at[slot])

    load_master.start()
    load_cot.start()
    load_act(1 - y, 2).start()
    load_act(y, 3).start()

    barrier = pltpu.get_barrier_semaphore()
    around = [along_first(0, 1), along_first(0, 3), along_last(0, 1), along_last(0, 3), partner]
    for other in around:
        pl.semaphore_signal(
            barrier, inc=1, device_id={"fsdp": other}, device_id_type=pl.DeviceIdType.MESH
        )
    load_master.wait()
    own_rows = pl.ds(pl.multiple_of(f * rows, rows), rows)
    for t in types:
        w[t, own_rows, :] = master[:, t * kv:(t + 1) * kv].astype(BF16)
    pl.semaphore_wait(barrier, len(around))
    for t in types:
        for d in ways:
            gp1(t, d).start()
    for t in types:
        for d in ways:
            gq1(t, 0, d).start()
        gy(t, 0).start()

    load_cot.wait()
    for t in types:
        cot_t[pl.ds(t * kv, kv), :] = cot[:, t * kv:(t + 1) * kv].T
    for t in types:
        acc[t] = jnp.zeros(acc.shape[1:], F32)
    load_act(1 - y, 2).wait()

    def make_parts(i):
        for t in types:
            plane, p = reduce_item(t, i)
            if t == 0:
                at = pl.multiple_of((plane * 4 + p) * cols, cols)
                right = act[:, pl.ds(at, cols)]
            else:
                right = jnp.concatenate(
                    [
                        act[:, pl.ds(pl.multiple_of(device(plane, q, p) * rows, rows), rows)]
                        for q in range(N)
                    ],
                    axis=1,
                )
            for m in range(2):
                at = m * kh
                prod = jnp.dot(
                    cot_t[pl.ds(t * kv + at, kh), :], right, preferred_element_type=F32
                ).astype(BF16)
                for q in range(N):
                    part[t, i, q, pl.ds(at, kh), :] = prod[:, q * rows:(q + 1) * rows]

    def add_half(t, i, d, got):
        at = pl.ds(d * kh, kh)
        q = (last_of[t] + sign(d)) % 4
        total = part[t, i, q, at, :].astype(F32) + got[...].astype(F32)
        part[t, i, q, at, :] = total.astype(BF16)

    def project(i):
        for t in types:
            plane, p = gather_item(t, i)
            if t == 0:
                at = pl.multiple_of((plane * 4 + p) * cols, cols)
                left = act[:, pl.ds(at, cols)]
                right = w[t, pl.ds(at, cols), :]
            else:
                spans = [
                    pl.ds(pl.multiple_of(device(plane, q, p) * rows, rows), rows) for q in range(N)
                ]
                left = jnp.concatenate([act[:, s] for s in spans], axis=1)
                right = jnp.concatenate([w[t, s, :] for s in spans], axis=0)
            acc[t] += jnp.dot(left, right, preferred_element_type=F32)

    def store_igrad(b):
        at = pl.ds(pl.multiple_of(b * cols, cols), cols)
        return pltpu.make_async_copy(igrad.at[:, at], igrad_hbm.at[0, :, at], store_sem.at[b])

    def input_grads(plane):
        def one(k, carry):
            b = plane * 4 + k
            at = pl.ds(pl.multiple_of(b * cols, cols), cols)
            total = None
            for t in types:
                term = lax.dot_general(
                    cot[:, t * kv:(t + 1) * kv], w[t, at, :], (((1,), (1,)), ((), ())),
                    preferred_element_type=F32,
                )
                total = term if total is None else total + term
            igrad[:, at] = total.astype(BF16)
            store_igrad(b).start()
            return carry

        lax.fori_loop(0, N, one, 0)

    def round_of(r, carry):
        @pl.when(r == 1)
        def _():
            for t in types:
                for d in (1, 0):
                    gp1(t, d).wait_recv()
                    gp2(t, d).start()
                gy(t, 1).start()
                gy(t, 3).start()

        @pl.when(r == 2)
        def _():
            for t in types:
                for d in ways:
                    gp2(t, d).wait_recv()
                gy(t, 2).start()

        @pl.when((r >= 4) & (r < ITEMS))
        def _():
            for t in types:
                gy(t, r % 4).wait_recv()

        @pl.when((r >= 1) & (r < ITEMS))
        def _():
            for t in types:
                for d in ways:
                    gq1(t, r, d).start()

        @pl.when(r == LAG_G)
        def _():
            load_act(y, 3).wait()

        @pl.when(r < ITEMS)
        def _():
            make_parts(r)
            for t in types:
                for d in ways:
                    rq1(t, r, d).start()

        @pl.when((r >= LAG_RQ2) & (r < ITEMS + LAG_RQ2))
        def _():
            i = r - LAG_RQ2
            for t in types:
                for d in ways:
                    rq1(t, i, d).wait_recv()
                    add_half(t, i, d, got_a.at[t, i, d])
                    rq2(t, i, d).start()

        @pl.when((r >= LAG_GQ2) & (r < ITEMS + LAG_GQ2))
        def _():
            i = r - LAG_GQ2
            for t in types:
                for d in ways:
                    gq1(t, i, d).wait_recv()
                    gq2(t, i, d).start()

        @pl.when((r >= LAG_RS) & (r < ITEMS + LAG_RS))
        def _():
            i = r - LAG_RS
            for t in types:
                for d in ways:
                    rq2(t, i, d).wait_recv()
                q = last_of[t]
                mine[t] = (
                    part[t, i, q].astype(F32)
                    + got_b[t, i, 0].astype(F32)
                    + got_b[t, i, 1].astype(F32)
                )

                @pl.when(i < 4)
                def _():
                    part[t, i, q] = mine[t].astype(BF16)
                    ry(t, i).start()

                @pl.when(i >= 4)
                def _():
                    ry(t, i % 4).wait_recv()
                    mine[t] += got_y[t, i % 4].astype(F32)

                @pl.when((i >= 4) & (i < 7))
                def _():
                    part[t, i, q] = mine[t].astype(BF16)

            @pl.when(i == 5)
            def _():
                for t in types:
                    for d in ways:
                        rp1(t, d).start()

            @pl.when(i == 6)
            def _():
                for t in types:
                    for d in ways:
                        rp1(t, d).wait_recv()
                        at = pl.ds(d * kh, kh)
                        k = 4 if d == 0 else 6
                        total = part[t, k, last_of[t], at, :].astype(F32)
                        total += got_pa[t, d].astype(F32)
                        part[t, k, last_of[t], at, :] = total.astype(BF16)
                        rp2(t, d).start()

        @pl.when((r >= LAG_G) & (r < ITEMS + LAG_G))
        def _():
            i = r - LAG_G
            for t in types:
                for d in ways:
                    gq2(t, i, d).wait_recv()
            project(i)

            @pl.when(i == 3)
            def _():
                input_grads(y)

            @pl.when(i == 7)
            def _():
                input_grads(1 - y)

        return carry

    lax.fori_loop(0, ROUNDS, round_of, 0)

    for t in types:
        out[:, t * kv:(t + 1) * kv] = acc[t].astype(BF16)
    store_out = pltpu.make_async_copy(out, out_hbm.at[0], store_sem.at[8])
    store_out.start()
    for t in types:
        for d in ways:
            rp2(t, d).wait_recv()
        total = mine[t] + got_pb[t, 0].astype(F32) + got_pb[t, 1].astype(F32)
        grad_ref[:, t * kv:(t + 1) * kv] = total.T

    for t in types:
        for d in ways:
            gp1(t, d).wait_send()
            gp2(t, d).wait_send()
            rp1(t, d).wait_send()
            rp2(t, d).wait_send()

    def drain_four(k, carry):
        for t in types:
            gy(t, k).wait_send()
            ry(t, k).wait_send()
        return carry

    def drain_eight(i, carry):
        for t in types:
            for d in ways:
                gq1(t, i, d).wait_send()
                gq2(t, i, d).wait_send()
                rq1(t, i, d).wait_send()
                rq2(t, i, d).wait_send()
        store_igrad(i).wait()
        return carry

    lax.fori_loop(0, N, drain_four, 0)
    lax.fori_loop(0, ITEMS, drain_eight, 0)
    store_out.wait()


def train_step(activations, cotangent, master):
    tok, width = activations.shape[1:]
    kv2 = cotangent.shape[2]
    rows = master.shape[1]
    kv, kh = kv2 // 2, kv2 // 4
    dma = pltpu.SemaphoreType.DMA
    sems = []
    for shape in ((2, 2), (2, 2), (2, 4), (2, 8, 2), (2, 8, 2)):
        sems += [dma(shape), dma(shape)]
    for shape in ((2, 8, 2), (2, 8, 2), (2, 4), (2, 2), (2, 2)):
        sems += [dma(shape), dma(shape)]
    hbm = pl.BlockSpec(memory_space=pl.ANY)
    return pl.pallas_call(
        train_kernel,
        out_shape=(
            jax.ShapeDtypeStruct((1, tok, kv2), BF16),
            jax.ShapeDtypeStruct((1, tok, width), BF16),
            jax.ShapeDtypeStruct((rows, kv2), F32),
        ),
        in_specs=[hbm, hbm, hbm],
        out_specs=(hbm, hbm, pl.BlockSpec(memory_space=pltpu.VMEM)),
        scratch_shapes=[
            pltpu.VMEM((tok, width), BF16),
            pltpu.VMEM((tok, kv2), BF16),
            pltpu.VMEM((kv2, tok), BF16),
            pltpu.VMEM((rows, kv2), F32),
            pltpu.VMEM((2, width, kv), BF16),
            pltpu.VMEM((2, 8, 4, kv, rows), BF16),
            pltpu.VMEM((2, 8, 2, kh, rows), BF16),
            pltpu.VMEM((2, 8, 2, kv, rows), BF16),
            pltpu.VMEM((2, 4, kv, rows), BF16),
            pltpu.VMEM((2, 2, kh, rows), BF16),
            pltpu.VMEM((2, 2, kv, rows), BF16),
            pltpu.VMEM((2, kv, rows), F32),
            pltpu.VMEM((2, tok, kv), F32),
            pltpu.VMEM((tok, kv2), BF16),
            pltpu.VMEM((tok, width), BF16),
            dma((4,)),
            dma((9,)),
            *sems,
        ],
        compiler_params=pltpu.CompilerParams(
            collective_id=0, has_side_effects=True, vmem_limit_bytes=56 * 2**20
        ),
        cost_estimate=pl.CostEstimate(
            flops=6 * tok * width * kv2, bytes_accessed=100 * 2**20, transcendentals=0
        ),
        name="train_step",
    )(activations, cotangent, master)


def shards(
    activations,
    kv_cotangent,
    kv_master,
    kv_first,
    kv_second,
    outer_params,
    local_params,
    outer_momentum,
):
    pseudo = outer_params - local_params[0]
    replicas = lax.axis_size("replica")
    summed_pseudo = lax.psum(pseudo.astype(BF16), "replica").astype(F32)

    projected, input_grad, summed = train_step(activations, kv_cotangent, kv_master)
    all_tokens = activations.shape[1] * lax.axis_size("fsdp")
    grad = summed * (1.0 / math.sqrt(all_tokens))
    new_master, new_first, new_second = adam_update(
        kv_master[0], kv_first[0], kv_second[0], grad
    )

    mean = summed_pseudo / replicas
    new_momentum = NESTEROV * outer_momentum + mean
    new_outer = outer_params - OUTER_RATE * (mean + NESTEROV * new_momentum)
    return (
        projected,
        input_grad,
        new_master[None],
        new_first[None],
        new_second[None],
        new_outer,
        new_momentum,
    )


def solution(mesh):
    row_split = P("replica", "fsdp", None)
    fragment = P(None, "fsdp", None)
    return jax.shard_map(
        shards,
        mesh=mesh,
        in_specs=(
            row_split,
            row_split,
            row_split,
            row_split,
            row_split,
            fragment,
            P("replica", None, "fsdp", None),
            fragment,
        ),
        out_specs=(row_split, row_split, row_split, row_split, row_split, fragment, fragment),
        check_vma=False,
    )
```

time: 336 us -> 116 us (0.35)
  waiting for transfers between devices: 286 us -> 0.02 us
  Pallas kernels: 0 us -> 90.8 us
  matrix products: 24.1 us -> 0 us
    reduce_scatter x1 -> x0, waiting for transfers between devices: 188 us -> none  [shards(): lax.psum_scatter(jnp.einsum('td,tk->dk', columns, cotangent, preferred_el...]
    pallas_call x0 -> x1, Pallas kernels: none -> 90.8 us  [train_step(): pl.pallas_call(train_kernel, out_shape=(jax.ShapeDtypeStruct((1, tok, kv2...]
    all_gather x1 -> x0, waiting for transfers between devices: 59.5 us -> none  [shards(): lax.all_gather(weights, 'fsdp', axis=0, tiled=True)]
    psum x1, waiting for transfers between devices: 38.9 us -> 0.01 us  [shards(): summed_pseudo = lax.psum(pseudo.astype(BF16), 'replica').astype(F32)]
    dot_general x3 -> x0, matrix products: 24.1 us -> none  [the longest x1 9.6 us: shards(): jnp.einsum('tk,dk->td', cotangent, lax.all_gather(weights, 'fsdp', axis=0...]
  transfers between devices with their start and end apart: 3 -> 1, of which waited for: 3 -> 0; matrix products, arithmetic and copies ran while one was open for 9% -> 2% of each run, Pallas kernels for 0% -> 78%
where the time goes in v1:
time: 116 us
  Pallas kernels  90.8 us (78%)
  between operations  14.1 us (12%)
  other arithmetic  7.96 us (7%)
  local copies, waits for them, and re-layouts  3.02 us (3%)
    pallas_call x1, Pallas kernels, train_step(): pl.pallas_call(train_kernel, out_shape=(jax.ShapeDtypeStruct((1, tok, kv2...  90.8 us
    unnamed x16, local copies, waits for them, and re-layouts  3.02 us
    sub x1, other arithmetic, shards(): new_outer = outer_params - OUTER_RATE * (mean + NESTEROV * new_momentum)  2.78 us
    broadcast_in_dim x1, other arithmetic, shards(): new_second[None]  2.75 us
    convert_element_type x1, other arithmetic, shards(): summed_pseudo = lax.psum(pseudo.astype(BF16), 'replica').astype(F32)  2.43 us
  transfers between devices with their start and end apart: 1, of which 0 were waited for; matrix products, arithmetic and copies ran while one was open for 2% of the time, Pallas kernels for 78%

profile of v1, /device:TPU:0, one launch (start us, length us, event | category | flops | bytes accessed | tf_op | source)
XLA Modules:
  0.0 116.0 jit_solution(11413636466695924585)
XLA Ops:
  7.2 0.0 all-reduce.2.cloned.1.call-start
  7.2 2.4 %fusion = bf16[2,32,4096]{2,1,0:T(8,128)(2,1)} fusion(f32[2,32,4096]{2,1,0:T(8,128)} %param.13, f32[1,2,32,4096]{3,2,1,0:T(8,128)} %param.14), kind=kLoop, calls=%fused_computation.1 | loop fusion | flops 524288 | bytes 2621440 | tf_op jit(solution)/shard_map/convert_element_type | solution.py:496
  9.6 0.0 all-reduce.2.cloned.1.call-update
  9.7 0.0 copy-start.4
  9.7 0.0 copy-start.5
  9.7 0.0 copy-start.6
  9.7 90.8 %train_step.1 = (bf16[1,512,1024]{2,1,0:T(8,128)(2,1)}, bf16[1,512,4096]{2,1,0:T(8,128)(2,1)}, f32[128,1024]{1,0:T(8,128)}) custom-call(bf16[1,512,4096]{2,1,0:T(8,128)(2,1)} %act_hbm.1, bf16[1,512,1024]{2,1,0:T(8,128)(2,1)} %cot_hbm.1, f32[1,128,1024]{2,1,0:T(8,128)} %master_hbm.1), custom_call_target="tpu_custom_call" | custom-call | flops 12884901888 | bytes 104857600 | tf_op jit(solution)/shard_map/train_step/pallas_call | solution.py:445
  100.5 0.0 copy-start.1
  100.5 0.0 copy-start.3
  100.6 0.0 copy-done.4
  100.6 0.0 copy-done.5
  100.6 0.0 copy-done.6
  100.6 0.0 copy-start.2
  100.6 2.7 %fusion.5 = (f32[1,128,1024]{2,1,0:T(8,128)}, f32[1,128,1024]{2,1,0:T(8,128)}, f32[1,128,1024]{2,1,0:T(8,128)}) fusion(f32[128,1024]{1,0:T(8,128)} %get-tuple-element.12, f32[1,128,1024]{2,1,0:T(8,128)S(1)} %copy-done.5, f32[1,128,1024]{2,1,0:T(8,128)S(1)} %copy-done.6, f32[1,128,1024]{2,1,0:T(8,128)S(1)} %copy-done.4), kind=kLoop, calls=%fused_computation.13 | loop fusion | flops 2097152 | bytes 3670016 | tf_op jit(solution)/shard_map/broadcast_in_dim | solution.py:513
  103.3 0.0 all-reduce.2.cloned.1.call-done
  103.3 0.0 copy-done.1
  103.3 0.0 copy-done.3
  103.3 0.0 copy-start
  103.4 2.8 %multiply_subtract_fusion = (f32[2,32,4096]{2,1,0:T(8,128)}, f32[2,32,4096]{2,1,0:T(8,128)}) fusion(f32[2,32,4096]{2,1,0:T(8,128)S(1)} %copy-done.1, bf16[2,32,4096]{2,1,0:T(8,128)(2,1)} %all-reduce.2.cloned.1.call-done, f32[2,32,4096]{2,1,0:T(8,128)S(1)} %copy-done.3), kind=kLoop, calls=%fused_computation.2 | loop fusion | flops 2097152 | bytes 4718592 | tf_op jit(solution)/shard_map/sub | solution.py:507
  106.1 0.0 copy-done.2
  106.1 1.0 copy.18
  107.1 0.0 copy-done
  107.1 2.0 %copy.19 = bf16[1,512,4096]{2,1,0:T(8,128)(2,1)} copy(bf16[1,512,4096]{2,1,0:T(8,128)(2,1)S(1)} %copy-done) | data formatting | bytes 8388608
Async XLA Ops:
  7.2 96.2 %all-reduce.2.cloned.1.call-start = ((), (), s32[]{:S(2)}) async-start(), calls=%async_computation | async-start | bytes 1048576 | tf_op jit(solution)/shard_map/psum | solution.py:496
  9.7 90.9 %copy-start.4 = (f32[1,128,1024]{2,1,0:T(8,128)S(1)}, f32[1,128,1024]{2,1,0:T(8,128)}, u32[]{:S(2)}) copy-start(f32[1,128,1024]{2,1,0:T(8,128)} %master_hbm.1) | copy-start | bytes 1572868
  9.7 90.9 %copy-start.5 = (f32[1,128,1024]{2,1,0:T(8,128)S(1)}, f32[1,128,1024]{2,1,0:T(8,128)}, u32[]{:S(2)}) copy-start(f32[1,128,1024]{2,1,0:T(8,128)} %param.12) | copy-start | bytes 1572868
  9.7 90.9 %copy-start.6 = (f32[1,128,1024]{2,1,0:T(8,128)S(1)}, f32[1,128,1024]{2,1,0:T(8,128)}, u32[]{:S(2)}) copy-start(f32[1,128,1024]{2,1,0:T(8,128)} %param.11) | copy-start | bytes 1572868
  100.5 2.8 %copy-start.1 = (f32[2,32,4096]{2,1,0:T(8,128)S(1)}, f32[2,32,4096]{2,1,0:T(8,128)}, u32[]{:S(2)}) copy-start(f32[2,32,4096]{2,1,0:T(8,128)} %param.13) | copy-start | bytes 3145732
  100.5 2.8 %copy-start.3 = (f32[2,32,4096]{2,1,0:T(8,128)S(1)}, f32[2,32,4096]{2,1,0:T(8,128)}, u32[]{:S(2)}) copy-start(f32[2,32,4096]{2,1,0:T(8,128)} %param.15) | copy-start | bytes 3145732
  100.6 5.6 %copy-start.2 = (bf16[1,512,1024]{2,1,0:T(8,128)(2,1)S(1)}, bf16[1,512,1024]{2,1,0:T(8,128)(2,1)}, u32[]{:S(2)}) copy-start(bf16[1,512,1024]{2,1,0:T(8,128)(2,1)} %get-tuple-element.25) | copy-start | bytes 3145732
  103.3 3.8 %copy-start = (bf16[1,512,4096]{2,1,0:T(8,128)(2,1)S(1)}, bf16[1,512,4096]{2,1,0:T(8,128)(2,1)}, u32[]{:S(2)}) copy-start(bf16[1,512,4096]{2,1,0:T(8,128)(2,1)} %get-tuple-element.26) | copy-start | bytes 12582916
Sparse Core Ops, SparseCore 0:
  11.1 44.3 all-reduce.1

commit v2 on v1

--- a/solution.py
+++ b/solution.py
@@ -18,6 +18,7 @@
 
 BF16 = jnp.bfloat16
 F32 = jnp.float32
+N_REPLICA = 4
 N = 4
 ITEMS = 2 * N
 LAG_RQ2 = 1
@@ -41,9 +42,14 @@
     act_hbm,
     cot_hbm,
     master_hbm,
+    outer_hbm,
+    local_hbm,
+    moment_hbm,
     out_hbm,
     igrad_hbm,
     grad_ref,
+    new_outer_hbm,
+    new_moment_hbm,
     act,
     cot,
     cot_t,
@@ -59,10 +65,19 @@
     acc,
     out,
     igrad,
+    outer,
+    local,
+    moment,
+    pseudo,
+    got_core,
+    chip_sum,
+    got_chip,
+    frag_total,
     load_sem,
     store_sem,
     gp1_s, gp1_r, gp2_s, gp2_r, gy_s, gy_r, gq1_s, gq1_r, gq2_s, gq2_r,
     rq1_s, rq1_r, rq2_s, rq2_r, ry_s, ry_r, rp1_s, rp1_r, rp2_s, rp2_r,
+    frag_s, frag_r,
 ):
     f = lax.axis_index("fsdp")
     y, x, z = f // 16, (f // 4) % 4, f % 4
@@ -165,6 +180,26 @@
             rp2_s.at[t, d], rp2_r.at[t, d], along_first(t, sign(d)),
         )
 
+    rep = lax.axis_index("replica")
+    core = rep % 2
+    other_core = rep + 1 - 2 * core
+    other_chip = rep + 2 - 4 * (rep // 2)
+
+    def frag_copy(k, src, dst, target):
+        return pltpu.make_async_remote_copy(
+            src_ref=src, dst_ref=dst, send_sem=frag_s.at[k], recv_sem=frag_r.at[k],
+            device_id={"replica": target}, device_id_type=pl.DeviceIdType.MESH,
+        )
+
+    def frag_core():
+        return frag_copy(0, pseudo, got_core, other_core)
+
+    def frag_chip():
+        return frag_copy(1, chip_sum, got_chip, other_chip)
+
+    def frag_back():
+        return frag_copy(2, frag_total.at[core], frag_total.at[core], other_core)
+
     types = (0, 1)
     ways = (0, 1)
 
@@ -180,6 +215,17 @@
     load_cot.start()
     load_act(1 - y, 2).start()
     load_act(y, 3).start()
+    load_frag = [
+        pltpu.make_async_copy(outer_hbm, outer, load_sem.at[4]),
+        pltpu.make_async_copy(local_hbm.at[0], local, load_sem.at[5]),
+        pltpu.make_async_copy(moment_hbm, moment, load_sem.at[6]),
+    ]
+    store_frag = [
+        pltpu.make_async_copy(outer, new_outer_hbm, store_sem.at[9]),
+        pltpu.make_async_copy(moment, new_moment_hbm, store_sem.at[10]),
+    ]
+    for load in load_frag:
+        load.start()
 
     barrier = pltpu.get_barrier_semaphore()
     around = [along_first(0, 1), along_first(0, 3), along_last(0, 1), along_last(0, 3), partner]
@@ -187,11 +233,15 @@
         pl.semaphore_signal(
             barrier, inc=1, device_id={"fsdp": other}, device_id_type=pl.DeviceIdType.MESH
         )
+    for other in (other_core, other_chip):
+        pl.semaphore_signal(
+            barrier, inc=1, device_id={"replica": other}, device_id_type=pl.DeviceIdType.MESH
+        )
     load_master.wait()
     own_rows = pl.ds(pl.multiple_of(f * rows, rows), rows)
     for t in types:
         w[t, own_rows, :] = master[:, t * kv:(t + 1) * kv].astype(BF16)
-    pl.semaphore_wait(barrier, len(around))
+    pl.semaphore_wait(barrier, len(around) + 2)
     for t in types:
         for d in ways:
             gp1(t, d).start()
@@ -271,6 +321,38 @@
 
         lax.fori_loop(0, N, one, 0)
 
+    def fragment_rounds(r):
+        @pl.when(r == 1)
+        def _():
+            for load in load_frag:
+                load.wait()
+            pseudo[...] = (outer[1 - core] - local[1 - core]).astype(BF16)
+            frag_core().start()
+
+        @pl.when(r == 2)
+        def _():
+            frag_core().wait_recv()
+            summed = outer[core] - local[core] + got_core[...].astype(F32)
+            chip_sum[...] = summed.astype(BF16)
+            frag_chip().start()
+
+        @pl.when(r == 5)
+        def _():
+            frag_chip().wait_recv()
+            frag_total[core] = chip_sum[...].astype(F32) + got_chip[...].astype(F32)
+            frag_back().start()
+
+        @pl.when(r == 6)
+        def _():
+            frag_back().wait_recv()
+            for layer in range(2):
+                mean = frag_total[layer] * (1.0 / N_REPLICA)
+                new_moment = NESTEROV * moment[layer] + mean
+                moment[layer] = new_moment
+                outer[layer] = outer[layer] - OUTER_RATE * (mean + NESTEROV * new_moment)
+            for store in store_frag:
+                store.start()
+
     def round_of(r, carry):
         @pl.when(r == 1)
         def _():
@@ -309,6 +391,8 @@
             for t in types:
                 for d in ways:
                     rq1(t, r, d).start()
+
+        fragment_rounds(r)
 
         @pl.when((r >= LAG_RQ2) & (r < ITEMS + LAG_RQ2))
         def _():
@@ -425,12 +509,16 @@
         store_igrad(i).wait()
         return carry
 
+    for copy in (frag_core(), frag_chip(), frag_back()):
+        copy.wait_send()
+    for store in store_frag:
+        store.wait()
     lax.fori_loop(0, N, drain_four, 0)
     lax.fori_loop(0, ITEMS, drain_eight, 0)
     store_out.wait()
 
 
-def train_step(activations, cotangent, master):
+def train_step(activations, cotangent, master, outer, local, moment):
     tok, width = activations.shape[1:]
     kv2 = cotangent.shape[2]
     rows = master.shape[1]
@@ -441,6 +529,8 @@
         sems += [dma(shape), dma(shape)]
     for shape in ((2, 8, 2), (2, 8, 2), (2, 4), (2, 2), (2, 2)):
         sems += [dma(shape), dma(shape)]
+    sems += [dma((3,)), dma((3,))]
+    layer = outer.shape[1:]
     hbm = pl.BlockSpec(memory_space=pl.ANY)
     return pl.pallas_call(
         train_kernel,
@@ -448,9 +538,11 @@
             jax.ShapeDtypeStruct((1, tok, kv2), BF16),
             jax.ShapeDtypeStruct((1, tok, width), BF16),
             jax.ShapeDtypeStruct((rows, kv2), F32),
+            jax.ShapeDtypeStruct(outer.shape, F32),
+            jax.ShapeDtypeStruct(outer.shape, F32),
         ),
-        in_specs=[hbm, hbm, hbm],
-        out_specs=(hbm, hbm, pl.BlockSpec(memory_space=pltpu.VMEM)),
+        in_specs=[hbm] * 6,
+        out_specs=(hbm, hbm, pl.BlockSpec(memory_space=pltpu.VMEM), hbm, hbm),
         scratch_shapes=[
             pltpu.VMEM((tok, width), BF16),
             pltpu.VMEM((tok, kv2), BF16),
@@ -467,8 +559,16 @@
             pltpu.VMEM((2, tok, kv), F32),
             pltpu.VMEM((tok, kv2), BF16),
             pltpu.VMEM((tok, width), BF16),
-            dma((4,)),
-            dma((9,)),
+            pltpu.VMEM((2, *layer), F32),
+            pltpu.VMEM((2, *layer), F32),
+            pltpu.VMEM((2, *layer), F32),
+            pltpu.VMEM(layer, BF16),
+            pltpu.VMEM(layer, BF16),
+            pltpu.VMEM(layer, BF16),
+            pltpu.VMEM(layer, BF16),
+            pltpu.VMEM((2, *layer), F32),
+            dma((7,)),
+            dma((11,)),
             *sems,
         ],
         compiler_params=pltpu.CompilerParams(
@@ -478,7 +578,7 @@
             flops=6 * tok * width * kv2, bytes_accessed=100 * 2**20, transcendentals=0
         ),
         name="train_step",
-    )(activations, cotangent, master)
+    )(activations, cotangent, master, outer, local, moment)
 
 
 def shards(
@@ -491,20 +591,15 @@
     local_params,
     outer_momentum,
 ):
-    pseudo = outer_params - local_params[0]
-    replicas = lax.axis_size("replica")
-    summed_pseudo = lax.psum(pseudo.astype(BF16), "replica").astype(F32)
-
-    projected, input_grad, summed = train_step(activations, kv_cotangent, kv_master)
+    projected, input_grad, summed, new_outer, new_momentum = train_step(
+        activations, kv_cotangent, kv_master, outer_params, local_params, outer_momentum
+    )
     all_tokens = activations.shape[1] * lax.axis_size("fsdp")
     grad = summed * (1.0 / math.sqrt(all_tokens))
     new_master, new_first, new_second = adam_update(
         kv_master[0], kv_first[0], kv_second[0], grad
     )
 
-    mean = summed_pseudo / replicas
-    new_momentum = NESTEROV * outer_momentum + mean
-    new_outer = outer_params - OUTER_RATE * (mean + NESTEROV * new_momentum)
     return (
         projected,
         input_grad,

time: 116 us -> 101 us (0.87)
  between operations: 14.1 us -> 0.7 us
  other arithmetic: 7.96 us -> 2.75 us
  local copies, waits for them, and re-layouts: 3.02 us -> 6.36 us
    unnamed x16, local copies, waits for them, and re-layouts: 3.02 us -> 6.36 us
    sub x1 -> x0, other arithmetic: 2.78 us -> none  [shards(): new_outer = outer_params - OUTER_RATE * (mean + NESTEROV * new_momentum)]
    convert_element_type x1 -> x0, other arithmetic: 2.43 us -> none  [shards(): summed_pseudo = lax.psum(pseudo.astype(BF16), 'replica').astype(F32)]
  transfers between devices with their start and end apart: 1 -> 0, of which waited for: 0 -> 0; matrix products, arithmetic and copies ran while one was open for 2% -> 0% of each run, Pallas kernels for 78% -> 0%
where the time goes in v2:
time: 101 us
  Pallas kernels  91 us (90%)
  local copies, waits for them, and re-layouts  6.36 us (6%)
  other arithmetic  2.75 us (3%)
    pallas_call x1, Pallas kernels, train_step(): pl.pallas_call(train_kernel, out_shape=(jax.ShapeDtypeStruct((1, tok, kv2...  91 us
    unnamed x16, local copies, waits for them, and re-layouts  6.36 us
    broadcast_in_dim x1, other arithmetic, shards(): new_second[None]  2.75 us

profile of v2, /device:TPU:0, one launch (start us, length us, event | category | flops | bytes accessed | tf_op | source)
XLA Modules:
  0.0 100.8 jit_solution(2547983081334148459)
XLA Ops:
  0.6 0.0 copy-start.3
  0.6 0.0 copy-start.4
  0.7 0.0 copy-start.5
  0.7 91.0 %train_step.1 = (bf16[1,512,1024]{2,1,0:T(8,128)(2,1)}, bf16[1,512,4096]{2,1,0:T(8,128)(2,1)}, f32[128,1024]{1,0:T(8,128)}, f32[2,32,4096]{2,1,0:T(8,128)}, f32[2,32,4096]{2,1,0:T(8,128)}) custom-call(bf16[1,512,4096]{2,1,0:T(8,128)(2,1)} %act_hbm.1, bf16[1,512,1024]{2,1,0:T(8,128)(2,1)} %cot_hbm.1, f32[1,128,1024]{2,1,0:T(8,128)} %master_hbm.1, ...), custom_call_target="tpu_custom_call" | custom-call | flops 12884901888 | bytes 104857600 | tf_op jit(solution)/shard_map/train_step/pallas_call | solution.py:535
  91.6 0.0 copy-start
  91.6 0.0 copy-done.3
  91.7 0.0 copy-done.4
  91.7 0.0 copy-done.5
  91.7 2.7 %fusion.4 = (f32[1,128,1024]{2,1,0:T(8,128)}, f32[1,128,1024]{2,1,0:T(8,128)}, f32[1,128,1024]{2,1,0:T(8,128)}) fusion(f32[128,1024]{1,0:T(8,128)} %get-tuple-element.14, f32[1,128,1024]{2,1,0:T(8,128)S(1)} %copy-done.4, f32[1,128,1024]{2,1,0:T(8,128)S(1)} %copy-done.5, f32[1,128,1024]{2,1,0:T(8,128)S(1)} %copy-done.3), kind=kLoop, calls=%fused_computation.8 | loop fusion | flops 2097152 | bytes 3670016 | tf_op jit(solution)/shard_map/broadcast_in_dim | solution.py:608
  94.4 2.3 %copy.19 = bf16[1,512,1024]{2,1,0:T(8,128)(2,1)} copy(bf16[1,512,1024]{2,1,0:T(8,128)(2,1)} %get-tuple-element.27) | data formatting | bytes 2097152
  96.7 0.0 copy-done
  96.7 0.0 copy-start.2
  96.7 0.0 copy-start.1
  96.7 2.1 %copy.20 = bf16[1,512,4096]{2,1,0:T(8,128)(2,1)} copy(bf16[1,512,4096]{2,1,0:T(8,128)(2,1)S(1)} %copy-done) | data formatting | bytes 8388608
  98.8 0.0 copy-done.2
  98.8 1.0 copy.21
  99.8 0.0 copy-done.1
  99.8 1.0 copy.22
Async XLA Ops:
  0.6 91.0 %copy-start.3 = (f32[1,128,1024]{2,1,0:T(8,128)S(1)}, f32[1,128,1024]{2,1,0:T(8,128)}, u32[]{:S(2)}) copy-start(f32[1,128,1024]{2,1,0:T(8,128)} %master_hbm.1) | copy-start | bytes 1572868
  0.6 91.0 %copy-start.4 = (f32[1,128,1024]{2,1,0:T(8,128)S(1)}, f32[1,128,1024]{2,1,0:T(8,128)}, u32[]{:S(2)}) copy-start(f32[1,128,1024]{2,1,0:T(8,128)} %param.12) | copy-start | bytes 1572868
  0.7 91.0 %copy-start.5 = (f32[1,128,1024]{2,1,0:T(8,128)S(1)}, f32[1,128,1024]{2,1,0:T(8,128)}, u32[]{:S(2)}) copy-start(f32[1,128,1024]{2,1,0:T(8,128)} %param.11) | copy-start | bytes 1572868
  91.6 5.1 %copy-start = (bf16[1,512,4096]{2,1,0:T(8,128)(2,1)S(1)}, bf16[1,512,4096]{2,1,0:T(8,128)(2,1)}, u32[]{:S(2)}) copy-start(bf16[1,512,4096]{2,1,0:T(8,128)(2,1)} %get-tuple-element.28) | copy-start | bytes 12582916
  96.7 2.1 %copy-start.2 = (f32[2,32,4096]{2,1,0:T(8,128)S(1)}, f32[2,32,4096]{2,1,0:T(8,128)}, u32[]{:S(2)}) copy-start(f32[2,32,4096]{2,1,0:T(8,128)} %get-tuple-element.32) | copy-start | bytes 3145732
  96.7 3.1 %copy-start.1 = (f32[2,32,4096]{2,1,0:T(8,128)S(1)}, f32[2,32,4096]{2,1,0:T(8,128)}, u32[]{:S(2)}) copy-start(f32[2,32,4096]{2,1,0:T(8,128)} %get-tuple-element.33) | copy-start | bytes 3145732

commit v3 on v2

--- a/solution.py
+++ b/solution.py
@@ -45,15 +45,18 @@
     outer_hbm,
     local_hbm,
     moment_hbm,
-    out_hbm,
-    igrad_hbm,
-    grad_ref,
-    new_outer_hbm,
-    new_moment_hbm,
+    first_hbm,
+    second_hbm,
+    out,
+    igrad,
+    master,
+    first,
+    second,
+    outer,
+    moment,
     act,
     cot,
     cot_t,
-    master,
     w,
     part,
     got_a,
@@ -63,18 +66,13 @@
     got_pb,
     mine,
     acc,
-    out,
-    igrad,
-    outer,
     local,
-    moment,
     pseudo,
     got_core,
     chip_sum,
     got_chip,
     frag_total,
     load_sem,
-    store_sem,
     gp1_s, gp1_r, gp2_s, gp2_r, gy_s, gy_r, gq1_s, gq1_r, gq2_s, gq2_r,
     rq1_s, rq1_r, rq2_s, rq2_r, ry_s, ry_r, rp1_s, rp1_r, rp2_s, rp2_r,
     frag_s, frag_r,
@@ -203,7 +201,7 @@
     types = (0, 1)
     ways = (0, 1)
 
-    load_master = pltpu.make_async_copy(master_hbm.at[0], master, load_sem.at[0])
+    load_master = pltpu.make_async_copy(master_hbm, master, load_sem.at[0])
     load_cot = pltpu.make_async_copy(cot_hbm.at[0], cot, load_sem.at[1])
     plane_cols = act.shape[1] // 2
 
@@ -220,10 +218,12 @@
         pltpu.make_async_copy(local_hbm.at[0], local, load_sem.at[5]),
         pltpu.make_async_copy(moment_hbm, moment, load_sem.at[6]),
     ]
-    store_frag = [
-        pltpu.make_async_copy(outer, new_outer_hbm, store_sem.at[9]),
-        pltpu.make_async_copy(moment, new_moment_hbm, store_sem.at[10]),
+    load_adam = [
+        pltpu.make_async_copy(first_hbm, first, load_sem.at[7]),
+        pltpu.make_async_copy(second_hbm, second, load_sem.at[8]),
     ]
+    for load in load_adam:
+        load.start()
     for load in load_frag:
         load.start()
 
@@ -240,7 +240,7 @@
     load_master.wait()
     own_rows = pl.ds(pl.multiple_of(f * rows, rows), rows)
     for t in types:
-        w[t, own_rows, :] = master[:, t * kv:(t + 1) * kv].astype(BF16)
+        w[t, own_rows, :] = master[0, :, t * kv:(t + 1) * kv].astype(BF16)
     pl.semaphore_wait(barrier, len(around) + 2)
     for t in types:
         for d in ways:
@@ -300,10 +300,6 @@
                 right = jnp.concatenate([w[t, s, :] for s in spans], axis=0)
             acc[t] += jnp.dot(left, right, preferred_element_type=F32)
 
-    def store_igrad(b):
-        at = pl.ds(pl.multiple_of(b * cols, cols), cols)
-        return pltpu.make_async_copy(igrad.at[:, at], igrad_hbm.at[0, :, at], store_sem.at[b])
-
     def input_grads(plane):
         def one(k, carry):
             b = plane * 4 + k
@@ -315,8 +311,7 @@
                     preferred_element_type=F32,
                 )
                 total = term if total is None else total + term
-            igrad[:, at] = total.astype(BF16)
-            store_igrad(b).start()
+            igrad[0, :, at] = total.astype(BF16)
             return carry
 
         lax.fori_loop(0, N, one, 0)
@@ -350,8 +345,6 @@
                 new_moment = NESTEROV * moment[layer] + mean
                 moment[layer] = new_moment
                 outer[layer] = outer[layer] - OUTER_RATE * (mean + NESTEROV * new_moment)
-            for store in store_frag:
-                store.start()
 
     def round_of(r, carry):
         @pl.when(r == 1)
@@ -477,14 +470,19 @@
     lax.fori_loop(0, ROUNDS, round_of, 0)
 
     for t in types:
-        out[:, t * kv:(t + 1) * kv] = acc[t].astype(BF16)
-    store_out = pltpu.make_async_copy(out, out_hbm.at[0], store_sem.at[8])
-    store_out.start()
+        out[0, :, t * kv:(t + 1) * kv] = acc[t].astype(BF16)
+    for load in load_adam:
+        load.wait()
+    tokens = act.shape[0] * 32
     for t in types:
         for d in ways:
             rp2(t, d).wait_recv()
         total = mine[t] + got_pb[t, 0].astype(F32) + got_pb[t, 1].astype(F32)
-        grad_ref[:, t * kv:(t + 1) * kv] = total.T
+        at = pl.ds(t * kv, kv)
+        master[0, :, at], first[0, :, at], second[0, :, at] = adam_update(
+            master[0, :, at], first[0, :, at], second[0, :, at],
+            total.T * (1.0 / math.sqrt(tokens)),
+        )
 
     for t in types:
         for d in ways:
@@ -506,19 +504,39 @@
                 gq2(t, i, d).wait_send()
                 rq1(t, i, d).wait_send()
                 rq2(t, i, d).wait_send()
-        store_igrad(i).wait()
         return carry
 
     for copy in (frag_core(), frag_chip(), frag_back()):
         copy.wait_send()
-    for store in store_frag:
-        store.wait()
     lax.fori_loop(0, N, drain_four, 0)
     lax.fori_loop(0, ITEMS, drain_eight, 0)
-    store_out.wait()
-
-
-def train_step(activations, cotangent, master, outer, local, moment):
+
+
+def write_kernel(*refs):
+    count = len(refs) // 2
+    sem = refs[-1]
+    copies = [
+        pltpu.make_async_copy(refs[k], refs[count + k], sem.at[k]) for k in range(count)
+    ]
+    for copy in copies:
+        copy.start()
+    for copy in copies:
+        copy.wait()
+
+
+def write_out(results):
+    return pl.pallas_call(
+        write_kernel,
+        out_shape=tuple(jax.ShapeDtypeStruct(r.shape, r.dtype) for r in results),
+        in_specs=[pl.BlockSpec(memory_space=pltpu.VMEM)] * len(results),
+        out_specs=tuple(pl.BlockSpec(memory_space=pl.ANY) for _ in results),
+        scratch_shapes=[pltpu.SemaphoreType.DMA((len(results),))],
+        compiler_params=pltpu.CompilerParams(vmem_limit_bytes=16 * 2**20),
+        name="write_out",
+    )(*results)
+
+
+def train_step(activations, cotangent, master, outer, local, moment, first, second):
     tok, width = activations.shape[1:]
     kv2 = cotangent.shape[2]
     rows = master.shape[1]
@@ -535,19 +553,20 @@
     return pl.pallas_call(
         train_kernel,
         out_shape=(
-            jax.ShapeDtypeStruct((1, tok, kv2), BF16),
-            jax.ShapeDtypeStruct((1, tok, width), BF16),
-            jax.ShapeDtypeStruct((rows, kv2), F32),
-            jax.ShapeDtypeStruct(outer.shape, F32),
-            jax.ShapeDtypeStruct(outer.shape, F32),
+            pltpu.VMEM((1, tok, kv2), BF16),
+            pltpu.VMEM((1, tok, width), BF16),
+            pltpu.VMEM((1, rows, kv2), F32),
+            pltpu.VMEM((1, rows, kv2), F32),
+            pltpu.VMEM((1, rows, kv2), F32),
+            pltpu.VMEM(outer.shape, F32),
+            pltpu.VMEM(outer.shape, F32),
         ),
-        in_specs=[hbm] * 6,
-        out_specs=(hbm, hbm, pl.BlockSpec(memory_space=pltpu.VMEM), hbm, hbm),
+        in_specs=[hbm] * 8,
+        out_specs=tuple(pl.BlockSpec(memory_space=pltpu.VMEM) for _ in range(7)),
         scratch_shapes=[
             pltpu.VMEM((tok, width), BF16),
             pltpu.VMEM((tok, kv2), BF16),
             pltpu.VMEM((kv2, tok), BF16),
-            pltpu.VMEM((rows, kv2), F32),
             pltpu.VMEM((2, width, kv), BF16),
             pltpu.VMEM((2, 8, 4, kv, rows), BF16),
             pltpu.VMEM((2, 8, 2, kh, rows), BF16),
@@ -557,28 +576,23 @@
             pltpu.VMEM((2, 2, kv, rows), BF16),
             pltpu.VMEM((2, kv, rows), F32),
             pltpu.VMEM((2, tok, kv), F32),
-            pltpu.VMEM((tok, kv2), BF16),
-            pltpu.VMEM((tok, width), BF16),
-            pltpu.VMEM((2, *layer), F32),
-            pltpu.VMEM((2, *layer), F32),
             pltpu.VMEM((2, *layer), F32),
             pltpu.VMEM(layer, BF16),
             pltpu.VMEM(layer, BF16),
             pltpu.VMEM(layer, BF16),
             pltpu.VMEM(layer, BF16),
             pltpu.VMEM((2, *layer), F32),
-            dma((7,)),
-            dma((11,)),
+            dma((9,)),
             *sems,
         ],
         compiler_params=pltpu.CompilerParams(
-            collective_id=0, has_side_effects=True, vmem_limit_bytes=56 * 2**20
+            collective_id=0, has_side_effects=True, vmem_limit_bytes=46 * 2**20
         ),
         cost_estimate=pl.CostEstimate(
             flops=6 * tok * width * kv2, bytes_accessed=100 * 2**20, transcendentals=0
         ),
         name="train_step",
-    )(activations, cotangent, master, outer, local, moment)
+    )(activations, cotangent, master, outer, local, moment, first, second)
 
 
 def shards(
@@ -591,23 +605,11 @@
     local_params,
     outer_momentum,
 ):
-    projected, input_grad, summed, new_outer, new_momentum = train_step(
-        activations, kv_cotangent, kv_master, outer_params, local_params, outer_momentum
-    )
-    all_tokens = activations.shape[1] * lax.axis_size("fsdp")
-    grad = summed * (1.0 / math.sqrt(all_tokens))
-    new_master, new_first, new_second = adam_update(
-        kv_master[0], kv_first[0], kv_second[0], grad
-    )
-
-    return (
-        projected,
-        input_grad,
-        new_master[None],
-        new_first[None],
-        new_second[None],
-        new_outer,
-        new_momentum,
+    return write_out(
+        train_step(
+            activations, kv_cotangent, kv_master, outer_params, local_params, outer_momentum,
+            kv_first, kv_second,
+        )
     )
 
 

time: 101 us -> 94.2 us (0.933)
  local copies, waits for them, and re-layouts: 6.36 us -> 0 us
  other arithmetic: 2.75 us -> 0 us
  Pallas kernels: 91 us -> 93.4 us
    unnamed x16 -> x0, local copies, waits for them, and re-layouts: 6.36 us -> none
    broadcast_in_dim x1 -> x0, other arithmetic: 2.75 us -> none  [shards(): new_second[None]]
    pallas_call x1 -> x2, Pallas kernels: 91 us -> 93.4 us  [the longest x1 89.9 us: train_step(): pl.pallas_call(train_kernel, out_shape=(pltpu.VMEM((1, tok, kv2), BF16),...]
where the time goes in v3:
time: 94.2 us; the launch traced here: 94.1 us
  Pallas kernels  93.4 us (99%)
    pallas_call x1, Pallas kernels, train_step(): pl.pallas_call(train_kernel, out_shape=(pltpu.VMEM((1, tok, kv2), BF16),...  89.9 us
    pallas_call x1, Pallas kernels, write_out(): pl.pallas_call(write_kernel, out_shape=tuple((jax.ShapeDtypeStruct(r.shap...  3.55 us

profile of v3, /device:TPU:0, one launch (start us, length us, event | category | flops | bytes accessed | tf_op | source)
XLA Modules:
  0.0 94.1 jit_solution(15690501135346786663)
XLA Ops:
  0.6 89.9 %train_step.1 = (bf16[1,512,1024]{2,1,0:T(8,128)(2,1)S(1)}, bf16[1,512,4096]{2,1,0:T(8,128)(2,1)S(1)}, f32[1,128,1024]{2,1,0:T(8,128)S(1)}, f32[1,128,1024]{2,1,...) custom-call(bf16[1,512,4096]{2,1,0:T(8,128)(2,1)} %act_hbm.1, ...), custom_call_target="tpu_custom_call" | custom-call | flops 12884901888 | bytes 104857600 | tf_op jit(solution)/shard_map/train_step/pallas_call | solution.py:553
  90.5 3.5 %write_out.1 = (bf16[1,512,1024]{2,1,0:T(8,128)(2,1)}, bf16[1,512,4096]{2,1,0:T(8,128)(2,1)}, f32[1,128,1024]{2,1,0:T(8,128)}, f32[1,128,1024]{2,1,0:T(8,128)}, ...) custom-call(bf16[1,512,1024]{2,1,0:T(8,128)(2,1)S(1)} %get-tuple-element.14.refs_0_, ...), custom_call_target="tpu_custom_call" | custom-call | tf_op jit(solution)/shard_map/write_out/pallas_call | solution.py:528

commit v4 on v3

--- a/solution.py
+++ b/solution.py
@@ -1,3 +1,4 @@
+import functools
 import math
 
 import jax
@@ -26,6 +27,8 @@
 LAG_GQ2 = 1
 LAG_G = 2
 ROUNDS = ITEMS + 2
+GATHER_LATE = 16
+REDUCE_EARLY = 64
 
 
 def adam_update(master, first, second, grad):
@@ -61,6 +64,7 @@
     part,
     got_a,
     got_b,
+    got_l,
     got_y,
     got_pa,
     got_pb,
@@ -75,29 +79,28 @@
     load_sem,
     gp1_s, gp1_r, gp2_s, gp2_r, gy_s, gy_r, gq1_s, gq1_r, gq2_s, gq2_r,
     rq1_s, rq1_r, rq2_s, rq2_r, ry_s, ry_r, rp1_s, rp1_r, rp2_s, rp2_r,
-    frag_s, frag_r,
+    frag_s, frag_r, gl_s, gl_r, rl_s, rl_r,
 ):
     f = lax.axis_index("fsdp")
     y, x, z = f // 16, (f // 4) % 4, f % 4
     first_of = (x, z)
     last_of = (z, x)
-    rows = w.shape[1] // 32
+    rows, kv = w.shape[4:]
     half = rows // 2
-    kv = w.shape[2]
-    kh = kv // 2
     cols = N * rows
+    keep_g = rows - GATHER_LATE
+    keep_r = kv - REDUCE_EARLY
 
     def device(yy, xx, zz):
         return (yy * 4 + xx) * 4 + zz
 
-    def block(t, yy, p, q):
-        return device(yy, p, q) if t == 0 else device(yy, q, p)
-
     def along_first(t, step):
-        return block(t, y, (first_of[t] + step) % 4, last_of[t])
+        p = (first_of[t] + step) % 4
+        return device(y, p, z) if t == 0 else device(y, x, p)
 
     def along_last(t, step):
-        return block(t, y, first_of[t], (last_of[t] + step) % 4)
+        q = (last_of[t] + step) % 4
+        return device(y, x, q) if t == 0 else device(y, q, z)
 
     partner = device(1 - y, x, z)
 
@@ -107,76 +110,98 @@
             device_id={"fsdp": target}, device_id_type=pl.DeviceIdType.MESH,
         )
 
-    def w_at(t, b, part_of=None):
-        if part_of is None:
-            return w.at[t, pl.ds(pl.multiple_of(b * rows, rows), rows)]
-        return w.at[t, pl.ds(pl.multiple_of(b * rows + part_of * half, half), half)]
+    def w_at(t, plane, p, q, start=0, stop=rows):
+        a, b = (p, q) if t == 0 else (q, p)
+        return w.at[t, plane, a, b, pl.ds(start, stop - start)]
 
     def sign(d):
         return 1 if d == 0 else 3
 
     def gp1(t, d):
-        own = w_at(t, f)
+        own = w_at(t, y, first_of[t], last_of[t])
         return send_to(own, own, gp1_s.at[t, d], gp1_r.at[t, d], along_first(t, sign(d)))
 
     def gp2(t, d):
-        ref = w_at(t, along_first(t, 4 - sign(d)), d)
+        ref = w_at(t, y, (first_of[t] + 4 - sign(d)) % 4, last_of[t], d * half, d * half + half)
         return send_to(ref, ref, gp2_s.at[t, d], gp2_r.at[t, d], along_first(t, sign(d)))
 
     def gy(t, k):
-        ref = w_at(t, along_first(t, k))
+        ref = w_at(t, y, (first_of[t] + k) % 4, last_of[t], 0, keep_g)
         return send_to(ref, ref, gy_s.at[t, k], gy_r.at[t, k], partner)
 
     def gather_item(t, i):
         plane = (y + i // 4) % 2
         return plane, (first_of[t] + i) % 4
 
-    def gq1(t, i, d):
+    def gl(t, k):
+        p = (first_of[t] + k) % 4
+        late = pl.ds(keep_g, GATHER_LATE)
+        ref = w.at[0, y, p, :, late] if t == 0 else w.at[1, y, :, p, late]
+        return send_to(ref, ref, gl_s.at[t, k], gl_r.at[t, k], partner)
+
+    def gq1(t, i, d, far):
         plane, p = gather_item(t, i)
-        ref = w_at(t, block(t, plane, p, last_of[t]))
+        ref = w_at(t, plane, p, last_of[t], 0, keep_g if far else rows)
         return send_to(ref, ref, gq1_s.at[t, i, d], gq1_r.at[t, i, d], along_last(t, sign(d)))
 
-    def gq2(t, i, d):
+    def gq2(t, i, d, far):
         plane, p = gather_item(t, i)
-        ref = w_at(t, block(t, plane, p, (last_of[t] + 4 - sign(d)) % 4), d)
+        end = keep_g if far else rows
+        q = (last_of[t] + 4 - sign(d)) % 4
+        ref = w_at(t, plane, p, q, d * half, half if d == 0 else end)
         return send_to(ref, ref, gq2_s.at[t, i, d], gq2_r.at[t, i, d], along_last(t, sign(d)))
 
     def reduce_item(t, i):
         plane = (y + 1 + i // 4) % 2
         return plane, (first_of[t] + i + 1) % 4
 
-    def part_at(t, i, q, part_of=None):
-        ref = part.at[t, i, q]
-        return ref if part_of is None else ref.at[pl.ds(part_of * kh, kh)]
-
-    def rq1(t, i, d):
+    def span(d, far):
+        if far:
+            cut = (keep_r - 4 * GATHER_LATE) // 2
+            return (0, cut) if d == 0 else (cut, keep_r - cut)
+        return d * (kv // 2), kv // 2
+
+    def rl(t, k):
+        ref = part.at[t, k, :, pl.ds(keep_r, REDUCE_EARLY)]
+        return send_to(ref, got_l.at[t, k], rl_s.at[t, k], rl_r.at[t, k], partner)
+
+    def rq1(t, i, d, far):
+        start, size = span(d, far)
         return send_to(
-            part_at(t, i, (last_of[t] + 2) % 4, d), got_a.at[t, i, d],
+            part.at[t, i, (last_of[t] + 2) % 4, pl.ds(start, size)],
+            got_a.at[t, i, d, pl.ds(0, size)],
             rq1_s.at[t, i, d], rq1_r.at[t, i, d], along_last(t, sign(d)),
         )
 
-    def rq2(t, i, d):
+    def rq2(t, i, d, far):
+        kept = pl.ds(0, keep_r if far else kv)
         return send_to(
-            part_at(t, i, (last_of[t] + sign(d)) % 4), got_b.at[t, i, d],
+            part.at[t, i, (last_of[t] + sign(d)) % 4, kept], got_b.at[t, i, d, kept],
             rq2_s.at[t, i, d], rq2_r.at[t, i, d], along_last(t, sign(d)),
         )
 
     def ry(t, k):
+        kept = pl.ds(0, keep_r)
         return send_to(
-            part_at(t, k, last_of[t]), got_y.at[t, k], ry_s.at[t, k], ry_r.at[t, k], partner
+            part.at[t, k, last_of[t], kept], got_y.at[t, k], ry_s.at[t, k], ry_r.at[t, k], partner
         )
 
     def rp1(t, d):
+        start, size = span(d, False)
         return send_to(
-            part_at(t, 5, last_of[t], d), got_pa.at[t, d],
+            part.at[t, 5, last_of[t], pl.ds(start, size)], got_pa.at[t, d],
             rp1_s.at[t, d], rp1_r.at[t, d], along_first(t, sign(d)),
         )
 
     def rp2(t, d):
         return send_to(
-            part_at(t, 4 if d == 0 else 6, last_of[t]), got_pb.at[t, d],
+            part.at[t, 4 if d == 0 else 6, last_of[t]], got_pb.at[t, d],
             rp2_s.at[t, d], rp2_r.at[t, d], along_first(t, sign(d)),
         )
+
+    def by_plane(first_far, i, body):
+        pl.when(i < N)(lambda: body(first_far))
+        pl.when(i >= N)(lambda: body(not first_far))
 
     rep = lax.axis_index("replica")
     core = rep % 2
@@ -209,10 +234,6 @@
         at = pl.ds(pl.multiple_of(plane * plane_cols, plane_cols), plane_cols)
         return pltpu.make_async_copy(act_hbm.at[0, :, at], act.at[:, at], load_sem.at[slot])
 
-    load_master.start()
-    load_cot.start()
-    load_act(1 - y, 2).start()
-    load_act(y, 3).start()
     load_frag = [
         pltpu.make_async_copy(outer_hbm, outer, load_sem.at[4]),
         pltpu.make_async_copy(local_hbm.at[0], local, load_sem.at[5]),
@@ -222,10 +243,9 @@
         pltpu.make_async_copy(first_hbm, first, load_sem.at[7]),
         pltpu.make_async_copy(second_hbm, second, load_sem.at[8]),
     ]
-    for load in load_adam:
-        load.start()
-    for load in load_frag:
-        load.start()
+    load_master.start()
+    load_cot.start()
+    load_act(1 - y, 2).start()
 
     barrier = pltpu.get_barrier_semaphore()
     around = [along_first(0, 1), along_first(0, 3), along_last(0, 1), along_last(0, 3), partner]
@@ -238,17 +258,19 @@
             barrier, inc=1, device_id={"replica": other}, device_id_type=pl.DeviceIdType.MESH
         )
     load_master.wait()
-    own_rows = pl.ds(pl.multiple_of(f * rows, rows), rows)
-    for t in types:
-        w[t, own_rows, :] = master[0, :, t * kv:(t + 1) * kv].astype(BF16)
+    for t in types:
+        w[t, y, x, z] = master[0, :, t * kv:(t + 1) * kv].astype(BF16)
     pl.semaphore_wait(barrier, len(around) + 2)
     for t in types:
         for d in ways:
             gp1(t, d).start()
     for t in types:
         for d in ways:
-            gq1(t, 0, d).start()
+            gq1(t, 0, d, False).start()
         gy(t, 0).start()
+    load_act(y, 3).start()
+    for load in load_frag + load_adam:
+        load.start()
 
     load_cot.wait()
     for t in types:
@@ -272,17 +294,18 @@
                     axis=1,
                 )
             for m in range(2):
-                at = m * kh
+                at = m * (kv // 2)
                 prod = jnp.dot(
-                    cot_t[pl.ds(t * kv + at, kh), :], right, preferred_element_type=F32
+                    cot_t[pl.ds(t * kv + at, kv // 2), :], right, preferred_element_type=F32
                 ).astype(BF16)
                 for q in range(N):
-                    part[t, i, q, pl.ds(at, kh), :] = prod[:, q * rows:(q + 1) * rows]
-
-    def add_half(t, i, d, got):
-        at = pl.ds(d * kh, kh)
+                    part[t, i, q, pl.ds(at, kv // 2), :] = prod[:, q * rows:(q + 1) * rows]
+
+    def add_half(t, i, d, far):
+        start, size = span(d, far)
+        at = pl.ds(start, size)
         q = (last_of[t] + sign(d)) % 4
-        total = part[t, i, q, at, :].astype(F32) + got[...].astype(F32)
+        total = part[t, i, q, at, :].astype(F32) + got_a[t, i, d, pl.ds(0, size)].astype(F32)
         part[t, i, q, at, :] = total.astype(BF16)
 
     def project(i):
@@ -291,14 +314,17 @@
             if t == 0:
                 at = pl.multiple_of((plane * 4 + p) * cols, cols)
                 left = act[:, pl.ds(at, cols)]
-                right = w[t, pl.ds(at, cols), :]
+                right = w[t, plane, p]
             else:
-                spans = [
-                    pl.ds(pl.multiple_of(device(plane, q, p) * rows, rows), rows) for q in range(N)
-                ]
-                left = jnp.concatenate([act[:, s] for s in spans], axis=1)
-                right = jnp.concatenate([w[t, s, :] for s in spans], axis=0)
-            acc[t] += jnp.dot(left, right, preferred_element_type=F32)
+                left = jnp.concatenate(
+                    [
+                        act[:, pl.ds(pl.multiple_of(device(plane, q, p) * rows, rows), rows)]
+                        for q in range(N)
+                    ],
+                    axis=1,
+                )
+                right = w[t, plane, :, p]
+            acc[t] += jnp.dot(left, right.reshape(cols, kv), preferred_element_type=F32)
 
     def input_grads(plane):
         def one(k, carry):
@@ -307,7 +333,8 @@
             total = None
             for t in types:
                 term = lax.dot_general(
-                    cot[:, t * kv:(t + 1) * kv], w[t, at, :], (((1,), (1,)), ((), ())),
+                    cot[:, t * kv:(t + 1) * kv], w[t, plane, k].reshape(cols, kv),
+                    (((1,), (1,)), ((), ())),
                     preferred_element_type=F32,
                 )
                 total = term if total is None else total + term
@@ -324,20 +351,20 @@
             pseudo[...] = (outer[1 - core] - local[1 - core]).astype(BF16)
             frag_core().start()
 
-        @pl.when(r == 2)
+        @pl.when(r == 3)
         def _():
             frag_core().wait_recv()
             summed = outer[core] - local[core] + got_core[...].astype(F32)
             chip_sum[...] = summed.astype(BF16)
             frag_chip().start()
 
-        @pl.when(r == 5)
+        @pl.when(r == 6)
         def _():
             frag_chip().wait_recv()
             frag_total[core] = chip_sum[...].astype(F32) + got_chip[...].astype(F32)
             frag_back().start()
 
-        @pl.when(r == 6)
+        @pl.when(r == 7)
         def _():
             frag_back().wait_recv()
             for layer in range(2):
@@ -370,9 +397,11 @@
 
         @pl.when((r >= 1) & (r < ITEMS))
         def _():
-            for t in types:
-                for d in ways:
-                    gq1(t, r, d).start()
+            @functools.partial(by_plane, False, r)
+            def _(far):
+                for t in types:
+                    for d in ways:
+                        gq1(t, r, d, far).start()
 
         @pl.when(r == LAG_G)
         def _():
@@ -381,55 +410,70 @@
         @pl.when(r < ITEMS)
         def _():
             make_parts(r)
-            for t in types:
-                for d in ways:
-                    rq1(t, r, d).start()
+
+            @functools.partial(by_plane, True, r)
+            def _(far):
+                for t in types:
+                    if not far:
+                        early = pl.ds(keep_r, REDUCE_EARLY)
+                        rl(t, r % N).wait_recv()
+                        both = part[t, r, :, early].astype(F32) + got_l[t, r % N].astype(F32)
+                        part[t, r, :, early] = both.astype(BF16)
+                    for d in ways:
+                        rq1(t, r, d, far).start()
+                    if far:
+                        rl(t, r).start()
 
         fragment_rounds(r)
 
         @pl.when((r >= LAG_RQ2) & (r < ITEMS + LAG_RQ2))
         def _():
             i = r - LAG_RQ2
-            for t in types:
-                for d in ways:
-                    rq1(t, i, d).wait_recv()
-                    add_half(t, i, d, got_a.at[t, i, d])
-                    rq2(t, i, d).start()
+
+            @functools.partial(by_plane, True, i)
+            def _(far):
+                for t in types:
+                    for d in ways:
+                        rq1(t, i, d, far).wait_recv()
+                        add_half(t, i, d, far)
+                        rq2(t, i, d, far).start()
 
         @pl.when((r >= LAG_GQ2) & (r < ITEMS + LAG_GQ2))
         def _():
             i = r - LAG_GQ2
-            for t in types:
-                for d in ways:
-                    gq1(t, i, d).wait_recv()
-                    gq2(t, i, d).start()
+
+            @functools.partial(by_plane, False, i)
+            def _(far):
+                for t in types:
+                    for d in ways:
+                        gq1(t, i, d, far).wait_recv()
+                        gq2(t, i, d, far).start()
 
         @pl.when((r >= LAG_RS) & (r < ITEMS + LAG_RS))
         def _():
             i = r - LAG_RS
-            for t in types:
-                for d in ways:
-                    rq2(t, i, d).wait_recv()
-                q = last_of[t]
-                mine[t] = (
-                    part[t, i, q].astype(F32)
-                    + got_b[t, i, 0].astype(F32)
-                    + got_b[t, i, 1].astype(F32)
-                )
-
-                @pl.when(i < 4)
-                def _():
-                    part[t, i, q] = mine[t].astype(BF16)
-                    ry(t, i).start()
-
-                @pl.when(i >= 4)
-                def _():
-                    ry(t, i % 4).wait_recv()
-                    mine[t] += got_y[t, i % 4].astype(F32)
-
-                @pl.when((i >= 4) & (i < 7))
-                def _():
-                    part[t, i, q] = mine[t].astype(BF16)
+
+            @functools.partial(by_plane, True, i)
+            def _(far):
+                for t in types:
+                    q = last_of[t]
+                    kept = pl.ds(0, keep_r if far else kv)
+                    for d in ways:
+                        rq2(t, i, d, far).wait_recv()
+                    total = part[t, i, q, kept].astype(F32)
+                    total += got_b[t, i, 0, kept].astype(F32)
+                    total += got_b[t, i, 1, kept].astype(F32)
+                    if far:
+                        part[t, i, q, kept] = total.astype(BF16)
+                        ry(t, i).start()
+                    else:
+                        ry(t, i % N).wait_recv()
+                        mine[t] = total
+                        mine[t, pl.ds(0, keep_r)] += got_y[t, i % N].astype(F32)
+
+                        @pl.when(i < 7)
+                        def _():
+                            part[t, i, q] = mine[t].astype(BF16)
 
             @pl.when(i == 5)
             def _():
@@ -442,7 +486,7 @@
                 for t in types:
                     for d in ways:
                         rp1(t, d).wait_recv()
-                        at = pl.ds(d * kh, kh)
+                        at = pl.ds(*span(d, False))
                         k = 4 if d == 0 else 6
                         total = part[t, k, last_of[t], at, :].astype(F32)
                         total += got_pa[t, d].astype(F32)
@@ -452,9 +496,17 @@
         @pl.when((r >= LAG_G) & (r < ITEMS + LAG_G))
         def _():
             i = r - LAG_G
-            for t in types:
-                for d in ways:
-                    gq2(t, i, d).wait_recv()
+
+            @functools.partial(by_plane, False, i)
+            def _(far):
+                for t in types:
+                    for d in ways:
+                        gq2(t, i, d, far).wait_recv()
+                    if far:
+                        gl(t, i % N).wait_recv()
+                    else:
+                        gl(t, i).start()
+
             project(i)
 
             @pl.when(i == 3)
@@ -491,25 +543,26 @@
             rp1(t, d).wait_send()
             rp2(t, d).wait_send()
 
-    def drain_four(k, carry):
+    def drain(k, carry):
         for t in types:
             gy(t, k).wait_send()
+            gl(t, k).wait_send()
+            rl(t, k).wait_send()
             ry(t, k).wait_send()
-        return carry
-
-    def drain_eight(i, carry):
-        for t in types:
             for d in ways:
-                gq1(t, i, d).wait_send()
-                gq2(t, i, d).wait_send()
-                rq1(t, i, d).wait_send()
-                rq2(t, i, d).wait_send()
+                gq1(t, k, d, False).wait_send()
+                gq2(t, k, d, False).wait_send()
+                rq1(t, k, d, True).wait_send()
+                rq2(t, k, d, True).wait_send()
+                gq1(t, k + N, d, True).wait_send()
+                gq2(t, k + N, d, True).wait_send()
+                rq1(t, k + N, d, False).wait_send()
+                rq2(t, k + N, d, False).wait_send()
         return carry
 
     for copy in (frag_core(), frag_chip(), frag_back()):
         copy.wait_send()
-    lax.fori_loop(0, N, drain_four, 0)
-    lax.fori_loop(0, ITEMS, drain_eight, 0)
+    lax.fori_loop(0, N, drain, 0)
 
 
 def write_kernel(*refs):
@@ -547,7 +600,8 @@
         sems += [dma(shape), dma(shape)]
     for shape in ((2, 8, 2), (2, 8, 2), (2, 4), (2, 2), (2, 2)):
         sems += [dma(shape), dma(shape)]
-    sems += [dma((3,)), dma((3,))]
+    for shape in ((3,), (2, 4), (2, 4)):
+        sems += [dma(shape), dma(shape)]
     layer = outer.shape[1:]
     hbm = pl.BlockSpec(memory_space=pl.ANY)
     return pl.pallas_call(
@@ -567,11 +621,12 @@
             pltpu.VMEM((tok, width), BF16),
             pltpu.VMEM((tok, kv2), BF16),
             pltpu.VMEM((kv2, tok), BF16),
-            pltpu.VMEM((2, width, kv), BF16),
+            pltpu.VMEM((2, 2, N, N, rows, kv), BF16),
             pltpu.VMEM((2, 8, 4, kv, rows), BF16),
-            pltpu.VMEM((2, 8, 2, kh, rows), BF16),
+            pltpu.VMEM((2, 8, 2, kv - kv // 4, rows), BF16),
             pltpu.VMEM((2, 8, 2, kv, rows), BF16),
-            pltpu.VMEM((2, 4, kv, rows), BF16),
+            pltpu.VMEM((2, 4, N, REDUCE_EARLY, rows), BF16),
+            pltpu.VMEM((2, 4, kv - REDUCE_EARLY, rows), BF16),
             pltpu.VMEM((2, 2, kh, rows), BF16),
             pltpu.VMEM((2, 2, kv, rows), BF16),
             pltpu.VMEM((2, kv, rows), F32),

time: 94.2 us -> 90.4 us (0.960)
  Pallas kernels: 93.4 us -> 89.6 us
    pallas_call x1, Pallas kernels: 89.9 us -> 86.1 us  [train_step(): pl.pallas_call(train_kernel, out_shape=(pltpu.VMEM((1, tok, kv2), BF16),...]
where the time goes in v4:
time: 90.4 us; the launch traced here: 90.3 us
  Pallas kernels  89.6 us (99%)
    pallas_call x1, Pallas kernels, train_step(): pl.pallas_call(train_kernel, out_shape=(pltpu.VMEM((1, tok, kv2), BF16),...  86.1 us
    pallas_call x1, Pallas kernels, write_out(): pl.pallas_call(write_kernel, out_shape=tuple((jax.ShapeDtypeStruct(r.shap...  3.55 us

profile of v4, /device:TPU:0, one launch (start us, length us, event | category | flops | bytes accessed | tf_op | source)
XLA Modules:
  0.0 90.3 jit_solution(10965740764132080013)
XLA Ops:
  0.6 86.1 %train_step.1 = (bf16[1,512,1024]{2,1,0:T(8,128)(2,1)S(1)}, bf16[1,512,4096]{2,1,0:T(8,128)(2,1)S(1)}, f32[1,128,1024]{2,1,0:T(8,128)S(1)}, f32[1,128,1024]{2,1,...) custom-call(bf16[1,512,4096]{2,1,0:T(8,128)(2,1)} %act_hbm.1, ...), custom_call_target="tpu_custom_call" | custom-call | flops 12884901888 | bytes 104857600 | tf_op jit(solution)/shard_map/train_step/pallas_call | solution.py:607
  86.7 3.5 %write_out.1 = (bf16[1,512,1024]{2,1,0:T(8,128)(2,1)}, bf16[1,512,4096]{2,1,0:T(8,128)(2,1)}, f32[1,128,1024]{2,1,0:T(8,128)}, f32[1,128,1024]{2,1,0:T(8,128)}, ...) custom-call(bf16[1,512,1024]{2,1,0:T(8,128)(2,1)S(1)} %get-tuple-element.14.refs_0_, ...), custom_call_target="tpu_custom_call" | custom-call | tf_op jit(solution)/shard_map/write_out/pallas_call | solution.py:581

commit v5 on v4

--- a/solution.py
+++ b/solution.py
@@ -22,11 +22,8 @@
 N_REPLICA = 4
 N = 4
 ITEMS = 2 * N
-LAG_RQ2 = 1
-LAG_RS = 2
-LAG_GQ2 = 1
-LAG_G = 2
-ROUNDS = ITEMS + 2
+SHIFT = 0
+ROUNDS = ITEMS + 1 + SHIFT
 GATHER_LATE = 16
 REDUCE_EARLY = 64
 
@@ -200,8 +197,11 @@
         )
 
     def by_plane(first_far, i, body):
-        pl.when(i < N)(lambda: body(first_far))
-        pl.when(i >= N)(lambda: body(not first_far))
+        if isinstance(i, int):
+            body(first_far if i < N else not first_far)
+        else:
+            pl.when(i < N)(lambda: body(first_far))
+            pl.when(i >= N)(lambda: body(not first_far))
 
     rep = lax.axis_index("replica")
     core = rep % 2
@@ -308,7 +308,24 @@
         total = part[t, i, q, at, :].astype(F32) + got_a[t, i, d, pl.ds(0, size)].astype(F32)
         part[t, i, q, at, :] = total.astype(BF16)
 
-    def project(i):
+    def project(i, steps, last=False):
+        for t in types:
+            plane, p = gather_item(t, i)
+            lefts, rights = [], []
+            for step in steps:
+                q = (last_of[t] + step) % 4
+                b = device(plane, p, q) if t == 0 else device(plane, q, p)
+                lefts.append(act[:, pl.ds(pl.multiple_of(b * rows, rows), rows)])
+                rights.append(w_at(t, plane, p, q)[...])
+            left = lefts[0] if len(lefts) == 1 else jnp.concatenate(lefts, axis=1)
+            right = rights[0] if len(rights) == 1 else jnp.concatenate(rights, axis=0)
+            term = jnp.dot(left, right, preferred_element_type=F32)
+            if last:
+                out[0, :, t * kv:(t + 1) * kv] = (acc[t] + term).astype(BF16)
+            else:
+                acc[t] += term
+
+    def project_all(i):
         for t in types:
             plane, p = gather_item(t, i)
             if t == 0:
@@ -326,8 +343,23 @@
                 right = w[t, plane, :, p]
             acc[t] += jnp.dot(left, right.reshape(cols, kv), preferred_element_type=F32)
 
-    def input_grads(plane):
-        def one(k, carry):
+    def input_grad_blocks(plane, places):
+        total = None
+        for t in types:
+            right = jnp.concatenate([w[t, plane, a, b] for a, b in places], axis=0)
+            term = lax.dot_general(
+                cot[:, t * kv:(t + 1) * kv], right, (((1,), (1,)), ((), ())),
+                preferred_element_type=F32,
+            )
+            total = term if total is None else total + term
+        total = total.astype(BF16)
+        for k, (a, b) in enumerate(places):
+            at = pl.ds(pl.multiple_of(device(plane, a, b) * rows, rows), rows)
+            igrad[0, :, at] = total[:, k * rows:(k + 1) * rows]
+
+    def input_grads(plane, start, count):
+        def one(step, carry):
+            k = (start + step) % 4
             b = plane * 4 + k
             at = pl.ds(pl.multiple_of(b * cols, cols), cols)
             total = None
@@ -341,7 +373,7 @@
             igrad[0, :, at] = total.astype(BF16)
             return carry
 
-        lax.fori_loop(0, N, one, 0)
+        lax.fori_loop(0, count, one, 0)
 
     def fragment_rounds(r):
         @pl.when(r == 1)
@@ -373,37 +405,54 @@
                 moment[layer] = new_moment
                 outer[layer] = outer[layer] - OUTER_RATE * (mean + NESTEROV * new_moment)
 
-    def round_of(r, carry):
-        @pl.when(r == 1)
-        def _():
+    def finish_item(i):
+        @functools.partial(by_plane, True, i)
+        def _(far):
             for t in types:
-                for d in (1, 0):
-                    gp1(t, d).wait_recv()
-                    gp2(t, d).start()
-                gy(t, 1).start()
-                gy(t, 3).start()
-
-        @pl.when(r == 2)
+                q = last_of[t]
+                kept = pl.ds(0, keep_r if far else kv)
+                for d in ways:
+                    rq2(t, i, d, far).wait_recv()
+                total = part[t, i, q, kept].astype(F32)
+                total += got_b[t, i, 0, kept].astype(F32)
+                total += got_b[t, i, 1, kept].astype(F32)
+                if far:
+                    part[t, i, q, kept] = total.astype(BF16)
+                    ry(t, i).start()
+                else:
+                    ry(t, i % N).wait_recv()
+                    mine[t] = total
+                    mine[t, pl.ds(0, keep_r)] += got_y[t, i % N].astype(F32)
+
+                    def keep():
+                        part[t, i, q] = mine[t].astype(BF16)
+
+                    if not isinstance(i, int):
+                        pl.when(i < 7)(keep)
+
+        if isinstance(i, int):
+            return
+
+        @pl.when(i == 5)
         def _():
             for t in types:
                 for d in ways:
-                    gp2(t, d).wait_recv()
-                gy(t, 2).start()
-
-        @pl.when((r >= 4) & (r < ITEMS))
+                    rp1(t, d).start()
+
+        @pl.when(i == 6)
         def _():
             for t in types:
-                gy(t, r % 4).wait_recv()
-
-        @pl.when((r >= 1) & (r < ITEMS))
-        def _():
-            @functools.partial(by_plane, False, r)
-            def _(far):
-                for t in types:
-                    for d in ways:
-                        gq1(t, r, d, far).start()
-
-        @pl.when(r == LAG_G)
+                for d in ways:
+                    rp1(t, d).wait_recv()
+                    at = pl.ds(*span(d, False))
+                    k = 4 if d == 0 else 6
+                    total = part[t, k, last_of[t], at, :].astype(F32)
+                    total += got_pa[t, d].astype(F32)
+                    part[t, k, last_of[t], at, :] = total.astype(BF16)
+                    rp2(t, d).start()
+
+    def round_of(r, carry):
+        @pl.when(r == 2)
         def _():
             load_act(y, 3).wait()
 
@@ -424,11 +473,39 @@
                     if far:
                         rl(t, r).start()
 
+        @pl.when(r == 1)
+        def _():
+            for t in types:
+                for d in (1, 0):
+                    gp1(t, d).wait_recv()
+                    gp2(t, d).start()
+                gy(t, 1).start()
+                gy(t, 3).start()
+
+        @pl.when(r == 2)
+        def _():
+            for t in types:
+                for d in ways:
+                    gp2(t, d).wait_recv()
+                gy(t, 2).start()
+
+        g = r - SHIFT
+
+        @pl.when((g >= 1) & (g < ITEMS))
+        def _():
+            @functools.partial(by_plane, False, g)
+            def _(far):
+                for t in types:
+                    if far:
+                        gy(t, g % N).wait_recv()
+                    for d in ways:
+                        gq1(t, g, d, far).start()
+
         fragment_rounds(r)
 
-        @pl.when((r >= LAG_RQ2) & (r < ITEMS + LAG_RQ2))
-        def _():
-            i = r - LAG_RQ2
+        @pl.when((r >= 1) & (r < ITEMS + 1))
+        def _():
+            i = r - 1
 
             @functools.partial(by_plane, True, i)
             def _(far):
@@ -438,9 +515,9 @@
                         add_half(t, i, d, far)
                         rq2(t, i, d, far).start()
 
-        @pl.when((r >= LAG_GQ2) & (r < ITEMS + LAG_GQ2))
-        def _():
-            i = r - LAG_GQ2
+        @pl.when((g >= 1) & (g < ITEMS + 1))
+        def _():
+            i = g - 1
 
             @functools.partial(by_plane, False, i)
             def _(far):
@@ -449,53 +526,13 @@
                         gq1(t, i, d, far).wait_recv()
                         gq2(t, i, d, far).start()
 
-        @pl.when((r >= LAG_RS) & (r < ITEMS + LAG_RS))
-        def _():
-            i = r - LAG_RS
-
-            @functools.partial(by_plane, True, i)
-            def _(far):
-                for t in types:
-                    q = last_of[t]
-                    kept = pl.ds(0, keep_r if far else kv)
-                    for d in ways:
-                        rq2(t, i, d, far).wait_recv()
-                    total = part[t, i, q, kept].astype(F32)
-                    total += got_b[t, i, 0, kept].astype(F32)
-                    total += got_b[t, i, 1, kept].astype(F32)
-                    if far:
-                        part[t, i, q, kept] = total.astype(BF16)
-                        ry(t, i).start()
-                    else:
-                        ry(t, i % N).wait_recv()
-                        mine[t] = total
-                        mine[t, pl.ds(0, keep_r)] += got_y[t, i % N].astype(F32)
-
-                        @pl.when(i < 7)
-                        def _():
-                            part[t, i, q] = mine[t].astype(BF16)
-
-            @pl.when(i == 5)
-            def _():
-                for t in types:
-                    for d in ways:
-                        rp1(t, d).start()
-
-            @pl.when(i == 6)
-            def _():
-                for t in types:
-                    for d in ways:
-                        rp1(t, d).wait_recv()
-                        at = pl.ds(*span(d, False))
-                        k = 4 if d == 0 else 6
-                        total = part[t, k, last_of[t], at, :].astype(F32)
-                        total += got_pa[t, d].astype(F32)
-                        part[t, k, last_of[t], at, :] = total.astype(BF16)
-                        rp2(t, d).start()
-
-        @pl.when((r >= LAG_G) & (r < ITEMS + LAG_G))
-        def _():
-            i = r - LAG_G
+        @pl.when((r >= 2) & (r < ITEMS + 2))
+        def _():
+            finish_item(r - 2)
+
+        @pl.when(g >= 2)
+        def _():
+            i = g - 2
 
             @functools.partial(by_plane, False, i)
             def _(far):
@@ -507,35 +544,49 @@
                     else:
                         gl(t, i).start()
 
-            project(i)
+            project_all(i)
 
             @pl.when(i == 3)
             def _():
-                input_grads(y)
-
-            @pl.when(i == 7)
-            def _():
-                input_grads(1 - y)
+                input_grads(y, 0, N)
 
         return carry
 
     lax.fori_loop(0, ROUNDS, round_of, 0)
 
+    def reduce_end():
+        if SHIFT == 0:
+            finish_item(7)
+        for load in load_adam:
+            load.wait()
+        tokens = act.shape[0] * 32
+        for t in types:
+            for d in ways:
+                rp2(t, d).wait_recv()
+            total = mine[t] + got_pb[t, 0].astype(F32) + got_pb[t, 1].astype(F32)
+            at = pl.ds(t * kv, kv)
+            master[0, :, at], first[0, :, at], second[0, :, at] = adam_update(
+                master[0, :, at], first[0, :, at], second[0, :, at],
+                total.T * (1.0 / math.sqrt(tokens)),
+            )
+
+    if SHIFT:
+        reduce_end()
     for t in types:
-        out[0, :, t * kv:(t + 1) * kv] = acc[t].astype(BF16)
-    for load in load_adam:
-        load.wait()
-    tokens = act.shape[0] * 32
+        gl(t, 3).wait_recv()
+    far_plane = 1 - y
+    xs, zs = [(x + k) % 4 for k in range(N)], [(z + k) % 4 for k in range(N)]
+    project(7, (0, 1, 3))
+    input_grads(far_plane, x, 2)
+    input_grad_blocks(far_plane, [(xs[2], zs[k]) for k in (0, 1, 2)])
+    input_grad_blocks(far_plane, [(xs[3], zs[k]) for k in (0, 1, 3)])
+    if not SHIFT:
+        reduce_end()
     for t in types:
         for d in ways:
-            rp2(t, d).wait_recv()
-        total = mine[t] + got_pb[t, 0].astype(F32) + got_pb[t, 1].astype(F32)
-        at = pl.ds(t * kv, kv)
-        master[0, :, at], first[0, :, at], second[0, :, at] = adam_update(
-            master[0, :, at], first[0, :, at], second[0, :, at],
-            total.T * (1.0 / math.sqrt(tokens)),
-        )
-
+            gq2(t, 7, d, True).wait_recv()
+    project(7, (2,), True)
+    input_grad_blocks(far_plane, [(xs[3], zs[2]), (xs[2], zs[3])])
     for t in types:
         for d in ways:
             gp1(t, d).wait_send()
@@ -568,9 +619,17 @@
 def write_kernel(*refs):
     count = len(refs) // 2
     sem = refs[-1]
-    copies = [
-        pltpu.make_async_copy(refs[k], refs[count + k], sem.at[k]) for k in range(count)
-    ]
+    copies = []
+    for k in range(count):
+        lines = refs[k].shape[1]
+        pieces = 4 if k == 1 else 2
+        for piece in range(pieces):
+            at = pl.ds(piece * (lines // pieces), lines // pieces)
+            copies.append(
+                pltpu.make_async_copy(
+                    refs[k].at[:, at], refs[count + k].at[:, at], sem.at[len(copies)]
+                )
+            )
     for copy in copies:
         copy.start()
     for copy in copies:
@@ -583,7 +642,7 @@
         out_shape=tuple(jax.ShapeDtypeStruct(r.shape, r.dtype) for r in results),
         in_specs=[pl.BlockSpec(memory_space=pltpu.VMEM)] * len(results),
         out_specs=tuple(pl.BlockSpec(memory_space=pl.ANY) for _ in results),
-        scratch_shapes=[pltpu.SemaphoreType.DMA((len(results),))],
+        scratch_shapes=[pltpu.SemaphoreType.DMA((2 * len(results) + 2,))],
         compiler_params=pltpu.CompilerParams(vmem_limit_bytes=16 * 2**20),
         name="write_out",
     )(*results)

time: 90.4 us -> 88.9 us (0.983)
  Pallas kernels: 89.6 us -> 88.1 us
    pallas_call x1, Pallas kernels: 86.1 us -> 84.5 us  [train_step(): pl.pallas_call(train_kernel, out_shape=(pltpu.VMEM((1, tok, kv2), BF16),...]
where the time goes in v5:
time: 88.9 us; the launch traced here: 88.8 us
  Pallas kernels  88.1 us (99%)
    pallas_call x1, Pallas kernels, train_step(): pl.pallas_call(train_kernel, out_shape=(pltpu.VMEM((1, tok, kv2), BF16),...  84.5 us
    pallas_call x1, Pallas kernels, write_out(): pl.pallas_call(write_kernel, out_shape=tuple((jax.ShapeDtypeStruct(r.shap...  3.58 us

profile of v5, /device:TPU:0, one launch (start us, length us, event | category | flops | bytes accessed | tf_op | source)
XLA Modules:
  0.0 88.8 jit_solution(3779391619151371938)
XLA Ops:
  0.6 84.5 %train_step.1 = (bf16[1,512,1024]{2,1,0:T(8,128)(2,1)S(1)}, bf16[1,512,4096]{2,1,0:T(8,128)(2,1)S(1)}, f32[1,128,1024]{2,1,0:T(8,128)S(1)}, f32[1,128,1024]{2,1,...) custom-call(bf16[1,512,4096]{2,1,0:T(8,128)(2,1)} %act_hbm.1, ...), custom_call_target="tpu_custom_call" | custom-call | flops 12884901888 | bytes 104857600 | tf_op jit(solution)/shard_map/train_step/pallas_call | solution.py:666
  85.2 3.6 %write_out.1 = (bf16[1,512,1024]{2,1,0:T(8,128)(2,1)}, bf16[1,512,4096]{2,1,0:T(8,128)(2,1)}, f32[1,128,1024]{2,1,0:T(8,128)}, f32[1,128,1024]{2,1,0:T(8,128)}, ...) custom-call(bf16[1,512,1024]{2,1,0:T(8,128)(2,1)S(1)} %get-tuple-element.14.refs_0_, ...), custom_call_target="tpu_custom_call" | custom-call | tf_op jit(solution)/shard_map/write_out/pallas_call | solution.py:640

commit v6 on v5

--- a/solution.py
+++ b/solution.py
@@ -47,7 +47,6 @@
     moment_hbm,
     first_hbm,
     second_hbm,
-    out,
     igrad,
     master,
     first,
@@ -56,17 +55,17 @@
     moment,
     act,
     cot,
+    w,
+    acc,
+    mine,
+    got_pb,
     cot_t,
-    w,
     part,
     got_a,
     got_b,
     got_l,
     got_y,
     got_pa,
-    got_pb,
-    mine,
-    acc,
     local,
     pseudo,
     got_core,
@@ -308,7 +307,7 @@
         total = part[t, i, q, at, :].astype(F32) + got_a[t, i, d, pl.ds(0, size)].astype(F32)
         part[t, i, q, at, :] = total.astype(BF16)
 
-    def project(i, steps, last=False):
+    def project(i, steps):
         for t in types:
             plane, p = gather_item(t, i)
             lefts, rights = [], []
@@ -319,11 +318,7 @@
                 rights.append(w_at(t, plane, p, q)[...])
             left = lefts[0] if len(lefts) == 1 else jnp.concatenate(lefts, axis=1)
             right = rights[0] if len(rights) == 1 else jnp.concatenate(rights, axis=0)
-            term = jnp.dot(left, right, preferred_element_type=F32)
-            if last:
-                out[0, :, t * kv:(t + 1) * kv] = (acc[t] + term).astype(BF16)
-            else:
-                acc[t] += term
+            acc[t] += jnp.dot(left, right, preferred_element_type=F32)
 
     def project_all(i):
         for t in types:
@@ -554,24 +549,6 @@
 
     lax.fori_loop(0, ROUNDS, round_of, 0)
 
-    def reduce_end():
-        if SHIFT == 0:
-            finish_item(7)
-        for load in load_adam:
-            load.wait()
-        tokens = act.shape[0] * 32
-        for t in types:
-            for d in ways:
-                rp2(t, d).wait_recv()
-            total = mine[t] + got_pb[t, 0].astype(F32) + got_pb[t, 1].astype(F32)
-            at = pl.ds(t * kv, kv)
-            master[0, :, at], first[0, :, at], second[0, :, at] = adam_update(
-                master[0, :, at], first[0, :, at], second[0, :, at],
-                total.T * (1.0 / math.sqrt(tokens)),
-            )
-
-    if SHIFT:
-        reduce_end()
     for t in types:
         gl(t, 3).wait_recv()
     far_plane = 1 - y
@@ -580,13 +557,14 @@
     input_grads(far_plane, x, 2)
     input_grad_blocks(far_plane, [(xs[2], zs[k]) for k in (0, 1, 2)])
     input_grad_blocks(far_plane, [(xs[3], zs[k]) for k in (0, 1, 3)])
-    if not SHIFT:
-        reduce_end()
+    for load in load_adam:
+        load.wait()
+    finish_item(7)
     for t in types:
         for d in ways:
+            rp2(t, d).wait_recv()
             gq2(t, 7, d, True).wait_recv()
-    project(7, (2,), True)
-    input_grad_blocks(far_plane, [(xs[3], zs[2]), (xs[2], zs[3])])
+
     for t in types:
         for d in ways:
             gp1(t, d).wait_send()
@@ -616,36 +594,101 @@
     lax.fori_loop(0, N, drain, 0)
 
 
-def write_kernel(*refs):
-    count = len(refs) // 2
-    sem = refs[-1]
-    copies = []
-    for k in range(count):
-        lines = refs[k].shape[1]
-        pieces = 4 if k == 1 else 2
-        for piece in range(pieces):
-            at = pl.ds(piece * (lines // pieces), lines // pieces)
-            copies.append(
-                pltpu.make_async_copy(
-                    refs[k].at[:, at], refs[count + k].at[:, at], sem.at[len(copies)]
-                )
-            )
-    for copy in copies:
+def finish_kernel(
+    igrad, master, first, second, outer, moment, act, cot, w, acc, mine, got_pb,
+    out_hbm, igrad_hbm, master_hbm, first_hbm, second_hbm, outer_hbm, moment_hbm,
+    out, last, new_master, new_first, new_second, sem,
+):
+    f = lax.axis_index("fsdp")
+    y, x, z = f // 16, (f // 4) % 4, f % 4
+    rows, kv = w.shape[4:]
+    cols = N * rows
+    plane = 1 - y
+    started = []
+
+    def put(src, dst):
+        copy = pltpu.make_async_copy(src, dst, sem.at[len(started)])
         copy.start()
-    for copy in copies:
+        started.append(copy)
+
+    def columns(start, size):
+        return pl.ds(pl.multiple_of(start, size), size)
+
+    def block(a, b):
+        return columns(((plane * 4 + a) * 4 + b) * rows, rows)
+
+    def put_igrad(at):
+        put(igrad.at[0, :, at], igrad_hbm.at[0, :, at])
+
+    xs, zs = [(x + k) % 4 for k in range(N)], [(z + k) % 4 for k in range(N)]
+    put(outer, outer_hbm)
+    put(moment, moment_hbm)
+    put_igrad(columns(y * N * cols, N * cols))
+    for k in (0, 1):
+        put_igrad(columns((plane * 4 + xs[k]) * cols, cols))
+    for k in (0, 1, 2):
+        put_igrad(block(xs[2], zs[k]))
+    for k in (0, 1, 3):
+        put_igrad(block(xs[3], zs[k]))
+
+    places = ((xs[3], zs[2]), (xs[2], zs[3]))
+    for t, (a, b) in enumerate(places):
+        at = slice(t * kv, (t + 1) * kv)
+        total = acc[t] + jnp.dot(act[:, block(a, b)], w[t, plane, a, b], preferred_element_type=F32)
+        out[:, at] = total.astype(BF16)
+        put(out.at[:, at], out_hbm.at[0, :, at])
+    total = None
+    for t in (0, 1):
+        right = jnp.concatenate([w[t, plane, a, b] for a, b in places], axis=0)
+        term = lax.dot_general(
+            cot[:, t * kv:(t + 1) * kv], right, (((1,), (1,)), ((), ())),
+            preferred_element_type=F32,
+        )
+        total = term if total is None else total + term
+    last[...] = total.astype(BF16)
+    for k, (a, b) in enumerate(places):
+        put(last.at[:, k * rows:(k + 1) * rows], igrad_hbm.at[0, :, block(a, b)])
+
+    tokens = act.shape[0] * 32
+    for t in (0, 1):
+        total = mine[t] + got_pb[t, 0].astype(F32) + got_pb[t, 1].astype(F32)
+        at = slice(t * kv, (t + 1) * kv)
+        new_master[:, at], new_first[:, at], new_second[:, at] = adam_update(
+            master[0, :, at], first[0, :, at], second[0, :, at],
+            total.T * (1.0 / math.sqrt(tokens)),
+        )
+        for src, dst in (
+            (new_master, master_hbm), (new_first, first_hbm), (new_second, second_hbm)
+        ):
+            put(src.at[:, at], dst.at[0, :, at])
+    for copy in started:
         copy.wait()
 
 
-def write_out(results):
+def finish(tok, kv2, rows, *held):
+    igrad, master, first, second, outer, moment = held[:6]
+    hbm = pl.BlockSpec(memory_space=pl.ANY)
+    results = [jax.ShapeDtypeStruct((1, tok, kv2), BF16)]
+    results += [
+        jax.ShapeDtypeStruct(r.shape, r.dtype)
+        for r in (igrad, master, first, second, outer, moment)
+    ]
     return pl.pallas_call(
-        write_kernel,
-        out_shape=tuple(jax.ShapeDtypeStruct(r.shape, r.dtype) for r in results),
-        in_specs=[pl.BlockSpec(memory_space=pltpu.VMEM)] * len(results),
-        out_specs=tuple(pl.BlockSpec(memory_space=pl.ANY) for _ in results),
-        scratch_shapes=[pltpu.SemaphoreType.DMA((2 * len(results) + 2,))],
+        finish_kernel,
+        out_shape=tuple(results),
+        in_specs=[pl.BlockSpec(memory_space=pltpu.VMEM)] * len(held),
+        out_specs=(hbm,) * len(results),
+        scratch_shapes=[
+            pltpu.VMEM((tok, kv2), BF16),
+            pltpu.VMEM((tok, 2 * rows), BF16),
+            pltpu.VMEM((rows, kv2), F32),
+            pltpu.VMEM((rows, kv2), F32),
+            pltpu.VMEM((rows, kv2), F32),
+            pltpu.SemaphoreType.DMA((21,)),
+        ],
         compiler_params=pltpu.CompilerParams(vmem_limit_bytes=16 * 2**20),
-        name="write_out",
-    )(*results)
+        name="finish",
+    )(*held)
 
 
 def train_step(activations, cotangent, master, outer, local, moment, first, second):
@@ -666,30 +709,29 @@
     return pl.pallas_call(
         train_kernel,
         out_shape=(
-            pltpu.VMEM((1, tok, kv2), BF16),
             pltpu.VMEM((1, tok, width), BF16),
             pltpu.VMEM((1, rows, kv2), F32),
             pltpu.VMEM((1, rows, kv2), F32),
             pltpu.VMEM((1, rows, kv2), F32),
             pltpu.VMEM(outer.shape, F32),
             pltpu.VMEM(outer.shape, F32),
+            pltpu.VMEM((tok, width), BF16),
+            pltpu.VMEM((tok, kv2), BF16),
+            pltpu.VMEM((2, 2, N, N, rows, kv), BF16),
+            pltpu.VMEM((2, tok, kv), F32),
+            pltpu.VMEM((2, kv, rows), F32),
+            pltpu.VMEM((2, 2, kv, rows), BF16),
         ),
         in_specs=[hbm] * 8,
-        out_specs=tuple(pl.BlockSpec(memory_space=pltpu.VMEM) for _ in range(7)),
+        out_specs=tuple(pl.BlockSpec(memory_space=pltpu.VMEM) for _ in range(12)),
         scratch_shapes=[
-            pltpu.VMEM((tok, width), BF16),
-            pltpu.VMEM((tok, kv2), BF16),
             pltpu.VMEM((kv2, tok), BF16),
-            pltpu.VMEM((2, 2, N, N, rows, kv), BF16),
             pltpu.VMEM((2, 8, 4, kv, rows), BF16),
             pltpu.VMEM((2, 8, 2, kv - kv // 4, rows), BF16),
             pltpu.VMEM((2, 8, 2, kv, rows), BF16),
             pltpu.VMEM((2, 4, N, REDUCE_EARLY, rows), BF16),
             pltpu.VMEM((2, 4, kv - REDUCE_EARLY, rows), BF16),
             pltpu.VMEM((2, 2, kh, rows), BF16),
-            pltpu.VMEM((2, 2, kv, rows), BF16),
-            pltpu.VMEM((2, kv, rows), F32),
-            pltpu.VMEM((2, tok, kv), F32),
             pltpu.VMEM((2, *layer), F32),
             pltpu.VMEM(layer, BF16),
             pltpu.VMEM(layer, BF16),
@@ -700,7 +742,7 @@
             *sems,
         ],
         compiler_params=pltpu.CompilerParams(
-            collective_id=0, has_side_effects=True, vmem_limit_bytes=46 * 2**20
+            collective_id=0, has_side_effects=True, vmem_limit_bytes=30 * 2**20
         ),
         cost_estimate=pl.CostEstimate(
             flops=6 * tok * width * kv2, bytes_accessed=100 * 2**20, transcendentals=0
@@ -719,12 +761,11 @@
     local_params,
     outer_momentum,
 ):
-    return write_out(
-        train_step(
-            activations, kv_cotangent, kv_master, outer_params, local_params, outer_momentum,
-            kv_first, kv_second,
-        )
+    held = train_step(
+        activations, kv_cotangent, kv_master, outer_params, local_params, outer_momentum,
+        kv_first, kv_second,
     )
+    return finish(activations.shape[1], kv_cotangent.shape[2], kv_master.shape[1], *held)
 
 
 def solution(mesh):

time: 88.9 us -> 87.5 us (0.984)
  Pallas kernels: 88.1 us -> 86.7 us
    pallas_call x2, Pallas kernels: 88.1 us -> 86.7 us  [the longest x1 83.1 us: train_step(): pl.pallas_call(train_kernel, out_shape=(pltpu.VMEM((1, tok, width), BF16)...]
where the time goes in v6:
time: 87.5 us; the launch traced here: 87.4 us
  Pallas kernels  86.7 us (99%)
    pallas_call x1, Pallas kernels, train_step(): pl.pallas_call(train_kernel, out_shape=(pltpu.VMEM((1, tok, width), BF16)...  83.1 us
    pallas_call x1, Pallas kernels, finish(): pl.pallas_call(finish_kernel, out_shape=tuple(results), in_specs=[pl.Bloc...  3.65 us

profile of v6, /device:TPU:0, one launch (start us, length us, event | category | flops | bytes accessed | tf_op | source)
XLA Modules:
  0.0 87.4 jit_solution(16505435049388181337)
XLA Ops:
  0.6 83.1 %train_step.1 = (bf16[1,512,4096]{2,1,0:T(8,128)(2,1)S(1)}, f32[1,128,1024]{2,1,0:T(8,128)S(1)}, f32[1,128,1024]{2,1,0:T(8,128)S(1)}, f32[1,128,1024]{2,1,0:T(8,...) custom-call(bf16[1,512,4096]{2,1,0:T(8,128)(2,1)} %act_hbm.1, ...), custom_call_target="tpu_custom_call" | custom-call | flops 12884901888 | bytes 104857600 | tf_op jit(solution)/shard_map/train_step/pallas_call | solution.py:709
  83.7 3.7 %finish.1 = (bf16[1,512,1024]{2,1,0:T(8,128)(2,1)}, bf16[1,512,4096]{2,1,0:T(8,128)(2,1)}, f32[1,128,1024]{2,1,0:T(8,128)}, f32[1,128,1024]{2,1,0:T(8,128)}, f32...) custom-call(bf16[1,512,4096]{2,1,0:T(8,128)(2,1)S(1)} %get-tuple-element.19.igrad, ...), custom_call_target="tpu_custom_call" | custom-call | tf_op jit(solution)/shard_map/finish/pallas_call | solution.py:676

commit v7 on v6

--- a/solution.py
+++ b/solution.py
@@ -24,6 +24,7 @@
 ITEMS = 2 * N
 SHIFT = 0
 ROUNDS = ITEMS + 1 + SHIFT
+PIECE_ROWS = 64
 GATHER_LATE = 16
 REDUCE_EARLY = 64
 
@@ -36,6 +37,23 @@
     update = first / first_fix / (jnp.sqrt(second / second_fix) + ADAM_EPSILON)
     master = master - INNER_RATE * (update + WEIGHT_DECAY * master)
     return (master, first, second)
+
+
+class Pieces:
+    def __init__(self, remote, shape):
+        self.remote, self.shape = remote, shape
+
+    def wait_recv(self):
+        self.remote(None).wait_recv()
+
+    def wait_send(self):
+        self.remote(None).wait_send()
+
+    def start(self):
+        count = self.shape[0]
+        step = 1 if len(self.shape) == 3 else PIECE_ROWS
+        for at in range(0, count, step):
+            self.remote(pl.ds(at, min(step, count - at))).start()
 
 
 def train_kernel(
@@ -101,10 +119,14 @@
     partner = device(1 - y, x, z)
 
     def send_to(src, dst, ss, rs, target):
-        return pltpu.make_async_remote_copy(
-            src_ref=src, dst_ref=dst, send_sem=ss, recv_sem=rs,
-            device_id={"fsdp": target}, device_id_type=pl.DeviceIdType.MESH,
-        )
+        def remote(at):
+            return pltpu.make_async_remote_copy(
+                src_ref=src if at is None else src.at[at], dst_ref=dst if at is None else dst.at[at],
+                send_sem=ss, recv_sem=rs,
+                device_id={"fsdp": target}, device_id_type=pl.DeviceIdType.MESH,
+            )
+
+        return Pieces(remote, src.shape)
 
     def w_at(t, plane, p, q, start=0, stop=rows):
         a, b = (p, q) if t == 0 else (q, p)
@@ -225,7 +247,12 @@
     types = (0, 1)
     ways = (0, 1)
 
-    load_master = pltpu.make_async_copy(master_hbm, master, load_sem.at[0])
+    def load_master(t):
+        at = pl.ds(t * kv, kv)
+        return pltpu.make_async_copy(
+            master_hbm.at[:, :, at], master.at[:, :, at], load_sem.at[(0, 9)[t]]
+        )
+
     load_cot = pltpu.make_async_copy(cot_hbm.at[0], cot, load_sem.at[1])
     plane_cols = act.shape[1] // 2
 
@@ -242,7 +269,8 @@
         pltpu.make_async_copy(first_hbm, first, load_sem.at[7]),
         pltpu.make_async_copy(second_hbm, second, load_sem.at[8]),
     ]
-    load_master.start()
+    for t in types:
+        load_master(t).start()
     load_cot.start()
     load_act(1 - y, 2).start()
 
@@ -256,15 +284,13 @@
         pl.semaphore_signal(
             barrier, inc=1, device_id={"replica": other}, device_id_type=pl.DeviceIdType.MESH
         )
-    load_master.wait()
     for t in types:
+        load_master(t).wait()
         w[t, y, x, z] = master[0, :, t * kv:(t + 1) * kv].astype(BF16)
-    pl.semaphore_wait(barrier, len(around) + 2)
-    for t in types:
+        if t == 0:
+            pl.semaphore_wait(barrier, len(around) + 2)
         for d in ways:
             gp1(t, d).start()
-    for t in types:
-        for d in ways:
             gq1(t, 0, d, False).start()
         gy(t, 0).start()
     load_act(y, 3).start()
@@ -378,7 +404,7 @@
             pseudo[...] = (outer[1 - core] - local[1 - core]).astype(BF16)
             frag_core().start()
 
-        @pl.when(r == 3)
+        @pl.when(r == 2)
         def _():
             frag_core().wait_recv()
             summed = outer[core] - local[core] + got_core[...].astype(F32)
@@ -738,7 +764,7 @@
             pltpu.VMEM(layer, BF16),
             pltpu.VMEM(layer, BF16),
             pltpu.VMEM((2, *layer), F32),
-            dma((9,)),
+            dma((10,)),
             *sems,
         ],
         compiler_params=pltpu.CompilerParams(

time: 87.5 us -> 87.6 us (level)
  no operation moved by 1% of the time
where the time goes in v7:
time: 87.6 us; the launch traced here: 87.5 us
  Pallas kernels  86.8 us (99%)
    pallas_call x1, Pallas kernels, train_step(): pl.pallas_call(train_kernel, out_shape=(pltpu.VMEM((1, tok, width), BF16)...  83.2 us
    pallas_call x1, Pallas kernels, finish(): pl.pallas_call(finish_kernel, out_shape=tuple(results), in_specs=[pl.Bloc...  3.65 us

profile of v7, /device:TPU:0, one launch (start us, length us, event | category | flops | bytes accessed | tf_op | source)
XLA Modules:
  0.0 87.5 jit_solution(16510773356481514948)
XLA Ops:
  0.6 83.2 %train_step.1 = (bf16[1,512,4096]{2,1,0:T(8,128)(2,1)S(1)}, f32[1,128,1024]{2,1,0:T(8,128)S(1)}, f32[1,128,1024]{2,1,0:T(8,128)S(1)}, f32[1,128,1024]{2,1,0:T(8,...) custom-call(bf16[1,512,4096]{2,1,0:T(8,128)(2,1)} %act_hbm.1, ...), custom_call_target="tpu_custom_call" | custom-call | flops 12884901888 | bytes 104857600 | tf_op jit(solution)/shard_map/train_step/pallas_call | solution.py:735
  83.8 3.7 %finish.1 = (bf16[1,512,1024]{2,1,0:T(8,128)(2,1)}, bf16[1,512,4096]{2,1,0:T(8,128)(2,1)}, f32[1,128,1024]{2,1,0:T(8,128)}, f32[1,128,1024]{2,1,0:T(8,128)}, f32...) custom-call(bf16[1,512,4096]{2,1,0:T(8,128)(2,1)S(1)} %get-tuple-element.19.igrad, ...), custom_call_target="tpu_custom_call" | custom-call | tf_op jit(solution)/shard_map/finish/pallas_call | solution.py:702
